TPU v7x, 512 devices: a whole 4x8x8 slice. The times are simulated.
512 devices in a mesh: depth: 8 (over y), lat: 32 (over z, x), freq: 2 (over core).
Axes of the slice: x: 4, y: 8, z: 8, core: 2. Of those that a mesh axis runs over, the one named last changes fastest.
Arguments:
- surface: bfloat16 [6, 2, 128, 32768], P('freq', None, None, 'lat'), may hold values from -6 to 6
- refl: float32 [8, 32768], P('depth', 'lat'), may hold values from -0.5 to 0.5
- pool: bfloat16 [8, 6, 8, 128, 256], P('depth', 'freq'), may hold values from -0.375 to 0.375
- tile_ids: int32 [8, 256, 10], P('depth', 'lat'), may hold values from 0 to 255, as said below
- block_ids: int32 [8, 256, 10], P('depth', 'lat'), may hold values from 0 to 7
- counts: int32 [8, 256], P('depth', 'lat'), may hold values from 1 to 10, as said below
Outputs:
- image: float32 [8, 32768], P('depth', 'lat')
Inputs may be any that keep to these rules, and one draw needn't show every extreme that they name: tile_ids[l, j, k] = (j + o) mod 256 for an offset o with -8 <= o <= 8; slot 0 names the row's own tile; in every level some row has all 10 slots live with offsets 8 at slot 1 and -8 at slot 2. Slots k >= counts[l, j] of row j are padding; in every level some row has all 10 slots live.
All inputs are finite; a program needn't handle non-finite values.
Results may differ from a plain program's by a relative error of at most 0.00055.
Values may be sent and summed in bfloat16 or wider, within the bound.
A program may use at most 128 MiB of HBM per device.

v0:
```python
import jax
import jax.numpy as jnp
from jax import lax
from jax.sharding import PartitionSpec as P

TILE = 128
TILE_DEV = 8


def extended_2(block, sides, width):
    for axis, dim in sides:
        count = lax.axis_size(axis)
        forward = [(i, i + 1) for i in range(count - 1)]
        forward.append((count - 1, 0))
        backward = [(target, source) for source, target in forward]
        low = lax.ppermute(
            lax.slice_in_dim(block, block.shape[dim] - width, None, axis=dim), axis, forward
        )
        high = lax.ppermute(lax.slice_in_dim(block, 0, width, axis=dim), axis, backward)
        block = jnp.concatenate([low, block, high], axis=dim)
    return block


def in_one_piece(arrays, axis, dim, along):
    columns = [a.reshape(*a.shape[:along], -1) for a in arrays]
    both = jnp.concatenate(columns, axis=along)
    whole, at, gathered = (lax.all_gather(both, axis, axis=dim, tiled=True), 0, [])
    for a, column in zip(arrays, columns):
        piece = whole[..., at : at + column.shape[along]]
        gathered.append(piece.reshape(*piece.shape[:along], *a.shape[along:]))
        at += column.shape[along]
    return tuple(gathered)


def copy_for_each(shard, axis):
    copies = jnp.broadcast_to(shard, (lax.axis_size(axis), *shard.shape))
    return lax.all_to_all(copies, axis, split_axis=0, concat_axis=0, tiled=True)


def in_order(parts, dim):
    parts = jnp.moveaxis(parts, 0, dim)
    shape = parts.shape
    return parts.reshape(*shape[:dim], shape[dim] * shape[dim + 1], *shape[dim + 2 :])


def gather_directly(shard, axis, dim):
    parts = copy_for_each(shard, axis)
    return in_order(parts, dim)


def cut_along(shard, dim, length):
    before, after = (shard.shape[:dim], shard.shape[dim + 1 :])
    return jnp.moveaxis(shard.reshape(*before, length, -1, *after), dim, 0)


def summed_on_arrival(shard, axis, dim):
    parts = cut_along(shard, dim, lax.axis_size(axis))
    arrived = lax.all_to_all(parts, axis, split_axis=0, concat_axis=0, tiled=True)
    return arrived.sum(axis=0)


def aperture_rim(wave_field):
    return extended_2(wave_field, (("lat", 3),), TILE_DEV * TILE)


def extrapolate(extended, pool_level, local_ids, block_level, count_level, refl_level):
    freqs_here = extended.shape[0]
    shot_rows = extended.shape[2]
    tile_rows = local_ids.shape[0]
    slot_total = local_ids.shape[1]
    tile_grid = extended.reshape(freqs_here, 2, shot_rows, -1, TILE)
    slot_live = (jnp.arange(slot_total)[None, :] < count_level[:, None]).astype(jnp.bfloat16)
    picked = jnp.take(tile_grid, local_ids, axis=3) * slot_live[None, None, None, :, :, None]
    chosen = jnp.take(pool_level, block_level, axis=1)
    product = jnp.einsum("fsarkt,frktc->rfsac", picked, chosen, preferred_element_type=jnp.float32)
    real_part = product[:, :, 0, :, :TILE] - product[:, :, 1, :, TILE:]
    imag_part = product[:, :, 0, :, TILE:] + product[:, :, 1, :, :TILE]
    row_scale = 1.0 / jnp.sqrt(count_level.astype(jnp.float32))
    rows_out = jnp.stack([real_part, imag_part], 2) * row_scale[:, None, None, None, None]
    wave_out = jnp.transpose(rows_out, (1, 2, 3, 0, 4)).reshape(
        freqs_here, 2, shot_rows, tile_rows * TILE
    )
    wave_out = wave_out * (1.0 - refl_level)
    return (wave_out.astype(jnp.bfloat16), jnp.sum(wave_out * wave_out, axis=(0, 1, 2)))


def per_device(surface, refl, pool, tile_ids, block_ids, counts):
    depth_index = lax.axis_index("depth")
    lat_index = lax.axis_index("lat")
    tile_count = TILE_DEV * lax.axis_size("lat")
    first_tile = lat_index * TILE_DEV - TILE_DEV
    freqs_here = surface.shape[0]
    shot_total = surface.shape[2]
    lateral_width = surface.shape[3]
    shot_rows = shot_total // lax.axis_size("depth")
    own_shots = lax.dynamic_slice_in_dim(surface, depth_index * shot_rows, shot_rows, 2)
    pool_all = lax.all_gather(pool, "depth", axis=0, tiled=True)
    ids_all, blocks_all, counts_all = in_one_piece((tile_ids, block_ids, counts), "depth", 0, 2)
    refl_all = gather_directly(refl, "depth", 0)
    level_total = pool_all.shape[0]

    def level_step(level_index, loop_state):
        wave_field, images = loop_state
        ids_here = lax.dynamic_index_in_dim(ids_all, level_index, 0, keepdims=False)
        local_level = jnp.mod(ids_here - first_tile, tile_count)
        pool_here = lax.dynamic_index_in_dim(pool_all, level_index, 0, keepdims=False)
        blocks_here = lax.dynamic_index_in_dim(blocks_all, level_index, 0, keepdims=False)
        counts_here = lax.dynamic_index_in_dim(counts_all, level_index, 0, keepdims=False)
        refl_here = lax.dynamic_index_in_dim(refl_all, level_index, 0, keepdims=False)
        handed, partial_value = extrapolate(
            aperture_rim(wave_field), pool_here, local_level, blocks_here, counts_here, refl_here
        )
        images = lax.dynamic_update_index_in_dim(images, partial_value, level_index, 0)
        return (handed, images)

    start_images = jnp.zeros((level_total, lateral_width), jnp.float32)
    loop_state = lax.fori_loop(0, level_total, level_step, (own_shots, start_images))
    image_local = summed_on_arrival(loop_state[1], "depth", 0)[0]
    summed = lax.psum(image_local, "freq")
    divisor = freqs_here * lax.axis_size("freq") * shot_total
    return (summed / divisor)[None, :]


def solution(mesh):
    placed = (
        P("freq", None, None, "lat"),
        P("depth", "lat"),
        P("depth", "freq", None, None, None),
        P("depth", "lat", None),
        P("depth", "lat", None),
        P("depth", "lat"),
    )
    return jax.shard_map(
        per_device, mesh=mesh, in_specs=placed, out_specs=P("depth", "lat"), check_vma=False
    )
```

profile of v0, /device:TPU:57, one launch (start us, length us, event | category | flops | bytes accessed | tf_op | source)
XLA Modules:
  0.0 456.6 jit_solution(3497054629939524282)
XLA Ops:
  8.6 6.3 %all-to-all-start = ((f32[8,1,1024]{2,1,0:T(1,128)}), f32[8,1,1024]{2,1,0:T(1,128)S(1)}, u32[]{:S(2)}, u32[]{:S(2)}) async-start(f32[8,1,1024]{2,1,0:T(1,128)} %broadcast_in_dim.88), calls=%async_computation | async-start | bytes 65536 | tf_op jit(solution)/shard_map/all_to_all | solution.py:37
  16.4 19.8 %all_gather.6 = s32[8,8,21]{2,1,0:T(8,128)S(1)} all-gather(s32[1,8,21]{2,1,0:T(8,128)S(1)} %pad_add_fusion), channel_id=1, replica_groups=mesh['depth'=8,'lat'=32,'freq'=2] {'depth'}, dimensions={0}, use_global_device_ids=true | all-gather | bytes 6048 | tf_op jit(solution)/shard_map/all_gather | solution.py:27
  37.7 110.3 %all-gather.2.cloned.1.call-done = bf16[8,3,8,128,256]{4,3,2,1,0:T(8,128)(2,1)} async-done(((bf16[1,3,8,128,256]{4,3,2,1,0:T(8,128)(2,1)}), bf16[8,3,8,128,256]{4,3,2,1,0:T(8,128)(2,1)}) %all-gather.2.cloned.1.call-update) | async-done | bytes 12582928 | tf_op jit(solution)/shard_map/all_gather | solution.py:97
  148.0 282.1 %while.17 = (s32[]{:T(128)}, bf16[3,2,16,1024]{3,2,1,0:T(8,128)(2,1)S(1)}, f32[8,1024]{1,0:T(8,128)}, s32[8,8,10]{2,1,0:T(8,128)S(1)}, s32[]{:T(128)}, /*index=5...) while((s32[]{:T(128)}, ...), condition=%wide.region_2.3_spmd, body=%wide.region_0.2_spmd.sunk | while | flops 515904960 | bytes 62015692 | solution.py:117
  148.0 7.8 %collective-permute-start = (bf16[3,2,16,1024]{3,2,1,0:T(8,128)(2,1)S(1)}, bf16[3,2,16,1024]{3,2,1,0:T(8,128)(2,1)S(1)}, u32[]{:S(2)}, u32[]{:S(2)}) collective-permute-start(bf16[3,2,16,1024]{3,2,1,0:T(8,128)(2,1)S(1)} %get-tuple-element.365), channel_id=1, source_target_pairs={{2,0},{4,2},{6,4},{8,6},{10,8},{12,10},{14,12},{16,14},{18,16},{20... | collective-permute-start | bytes 589832 | tf_op jit(solution)/shard_map/while/body/eval_jaxpr/ppermute | solution.py:19
  162.1 8.2 %gather_fusion = bf16[80,3,128,256]{3,2,1,0:T(8,128)(2,1)} fusion(bf16[3,8,128,256]{3,2,1,0:T(8,128)(2,1)S(1)} %dynamic-slice_bitcast_fusion.2, s32[1024]{0:T(1024)S(1)} %pad_clamp_fusion.4), kind=kCustom, calls=%fused_computation.1.clone.1 | custom fusion | bytes 31457600 | tf_op jit(solution)/shard_map/while/body/eval_jaxpr/jit(_take)/gather | solution.py:74
  174.4 8.0 %fusion.30 = f32[8,3,2,16,256]{4,3,2,1,0:T(8,128)S(1)} fusion(bf16[8,10,3,128,256]{4,3,2,1,0:T(8,128)(2,1)} %bitcast.98, pred[8,10]{1,0:T(8,128)(4,1)S(1)} %copy-done.5, bf16[8,10,3,2,16,128]{5,4,3,2,1,0:T(8,128)(2,1)} %bitcast.99, pred[8,10]{1,0:T(8,128)(4,1)S(1)} %copy-done.6, bf16[8,10]{1,0:T(8,128)(2,1)S(1)} %fusion.29), kind=kOutput, calls=%fused_computation.8.clone.1 | convolution fusion | flops 513146880 | bytes 18481472 | tf_op jit(solution)/shard_map/while/body/eval_jaxpr/fsarkt,frktc->rfsac/dot_general | solution.py:75
  184.2 6.7 %collective-permute-start = (bf16[3,2,16,1024]{3,2,1,0:T(8,128)(2,1)S(1)}, bf16[3,2,16,1024]{3,2,1,0:T(8,128)(2,1)S(1)}, u32[]{:S(2)}, u32[]{:S(2)}) collective-permute-start(bf16[3,2,16,1024]{3,2,1,0:T(8,128)(2,1)S(1)} %get-tuple-element.365), channel_id=1, source_target_pairs={{2,0},{4,2},{6,4},{8,6},{10,8},{12,10},{14,12},{16,14},{18,16},{20... | collective-permute-start | bytes 589832 | tf_op jit(solution)/shard_map/while/body/eval_jaxpr/ppermute | solution.py:19
  197.2 8.2 %gather_fusion = bf16[80,3,128,256]{3,2,1,0:T(8,128)(2,1)} fusion(bf16[3,8,128,256]{3,2,1,0:T(8,128)(2,1)S(1)} %dynamic-slice_bitcast_fusion.2, s32[1024]{0:T(1024)S(1)} %pad_clamp_fusion.4), kind=kCustom, calls=%fused_computation.1.clone.1 | custom fusion | bytes 31457600 | tf_op jit(solution)/shard_map/while/body/eval_jaxpr/jit(_take)/gather | solution.py:74
  207.2 2.4 gather_fusion.1
  209.6 8.0 %fusion.30 = f32[8,3,2,16,256]{4,3,2,1,0:T(8,128)S(1)} fusion(bf16[8,10,3,128,256]{4,3,2,1,0:T(8,128)(2,1)} %bitcast.98, pred[8,10]{1,0:T(8,128)(4,1)S(1)} %copy-done.5, bf16[8,10,3,2,16,128]{5,4,3,2,1,0:T(8,128)(2,1)} %bitcast.99, pred[8,10]{1,0:T(8,128)(4,1)S(1)} %copy-done.6, bf16[8,10]{1,0:T(8,128)(2,1)S(1)} %fusion.29), kind=kOutput, calls=%fused_computation.8.clone.1 | convolution fusion | flops 513146880 | bytes 18481472 | tf_op jit(solution)/shard_map/while/body/eval_jaxpr/fsarkt,frktc->rfsac/dot_general | solution.py:75
  219.4 6.7 %collective-permute-start = (bf16[3,2,16,1024]{3,2,1,0:T(8,128)(2,1)S(1)}, bf16[3,2,16,1024]{3,2,1,0:T(8,128)(2,1)S(1)}, u32[]{:S(2)}, u32[]{:S(2)}) collective-permute-start(bf16[3,2,16,1024]{3,2,1,0:T(8,128)(2,1)S(1)} %get-tuple-element.365), channel_id=1, source_target_pairs={{2,0},{4,2},{6,4},{8,6},{10,8},{12,10},{14,12},{16,14},{18,16},{20... | collective-permute-start | bytes 589832 | tf_op jit(solution)/shard_map/while/body/eval_jaxpr/ppermute | solution.py:19
  232.3 8.2 %gather_fusion = bf16[80,3,128,256]{3,2,1,0:T(8,128)(2,1)} fusion(bf16[3,8,128,256]{3,2,1,0:T(8,128)(2,1)S(1)} %dynamic-slice_bitcast_fusion.2, s32[1024]{0:T(1024)S(1)} %pad_clamp_fusion.4), kind=kCustom, calls=%fused_computation.1.clone.1 | custom fusion | bytes 31457600 | tf_op jit(solution)/shard_map/while/body/eval_jaxpr/jit(_take)/gather | solution.py:74
  244.7 8.0 %fusion.30 = f32[8,3,2,16,256]{4,3,2,1,0:T(8,128)S(1)} fusion(bf16[8,10,3,128,256]{4,3,2,1,0:T(8,128)(2,1)} %bitcast.98, pred[8,10]{1,0:T(8,128)(4,1)S(1)} %copy-done.5, bf16[8,10,3,2,16,128]{5,4,3,2,1,0:T(8,128)(2,1)} %bitcast.99, pred[8,10]{1,0:T(8,128)(4,1)S(1)} %copy-done.6, bf16[8,10]{1,0:T(8,128)(2,1)S(1)} %fusion.29), kind=kOutput, calls=%fused_computation.8.clone.1 | convolution fusion | flops 513146880 | bytes 18481472 | tf_op jit(solution)/shard_map/while/body/eval_jaxpr/fsarkt,frktc->rfsac/dot_general | solution.py:75
  254.5 6.7 %collective-permute-start = (bf16[3,2,16,1024]{3,2,1,0:T(8,128)(2,1)S(1)}, bf16[3,2,16,1024]{3,2,1,0:T(8,128)(2,1)S(1)}, u32[]{:S(2)}, u32[]{:S(2)}) collective-permute-start(bf16[3,2,16,1024]{3,2,1,0:T(8,128)(2,1)S(1)} %get-tuple-element.365), channel_id=1, source_target_pairs={{2,0},{4,2},{6,4},{8,6},{10,8},{12,10},{14,12},{16,14},{18,16},{20... | collective-permute-start | bytes 589832 | tf_op jit(solution)/shard_map/while/body/eval_jaxpr/ppermute | solution.py:19
  267.4 8.2 %gather_fusion = bf16[80,3,128,256]{3,2,1,0:T(8,128)(2,1)} fusion(bf16[3,8,128,256]{3,2,1,0:T(8,128)(2,1)S(1)} %dynamic-slice_bitcast_fusion.2, s32[1024]{0:T(1024)S(1)} %pad_clamp_fusion.4), kind=kCustom, calls=%fused_computation.1.clone.1 | custom fusion | bytes 31457600 | tf_op jit(solution)/shard_map/while/body/eval_jaxpr/jit(_take)/gather | solution.py:74
  279.8 8.0 %fusion.30 = f32[8,3,2,16,256]{4,3,2,1,0:T(8,128)S(1)} fusion(bf16[8,10,3,128,256]{4,3,2,1,0:T(8,128)(2,1)} %bitcast.98, pred[8,10]{1,0:T(8,128)(4,1)S(1)} %copy-done.5, bf16[8,10,3,2,16,128]{5,4,3,2,1,0:T(8,128)(2,1)} %bitcast.99, pred[8,10]{1,0:T(8,128)(4,1)S(1)} %copy-done.6, bf16[8,10]{1,0:T(8,128)(2,1)S(1)} %fusion.29), kind=kOutput, calls=%fused_computation.8.clone.1 | convolution fusion | flops 513146880 | bytes 18481472 | tf_op jit(solution)/shard_map/while/body/eval_jaxpr/fsarkt,frktc->rfsac/dot_general | solution.py:75
  289.6 6.7 %collective-permute-start = (bf16[3,2,16,1024]{3,2,1,0:T(8,128)(2,1)S(1)}, bf16[3,2,16,1024]{3,2,1,0:T(8,128)(2,1)S(1)}, u32[]{:S(2)}, u32[]{:S(2)}) collective-permute-start(bf16[3,2,16,1024]{3,2,1,0:T(8,128)(2,1)S(1)} %get-tuple-element.365), channel_id=1, source_target_pairs={{2,0},{4,2},{6,4},{8,6},{10,8},{12,10},{14,12},{16,14},{18,16},{20... | collective-permute-start | bytes 589832 | tf_op jit(solution)/shard_map/while/body/eval_jaxpr/ppermute | solution.py:19
  302.6 8.2 %gather_fusion = bf16[80,3,128,256]{3,2,1,0:T(8,128)(2,1)} fusion(bf16[3,8,128,256]{3,2,1,0:T(8,128)(2,1)S(1)} %dynamic-slice_bitcast_fusion.2, s32[1024]{0:T(1024)S(1)} %pad_clamp_fusion.4), kind=kCustom, calls=%fused_computation.1.clone.1 | custom fusion | bytes 31457600 | tf_op jit(solution)/shard_map/while/body/eval_jaxpr/jit(_take)/gather | solution.py:74
  314.9 8.0 %fusion.30 = f32[8,3,2,16,256]{4,3,2,1,0:T(8,128)S(1)} fusion(bf16[8,10,3,128,256]{4,3,2,1,0:T(8,128)(2,1)} %bitcast.98, pred[8,10]{1,0:T(8,128)(4,1)S(1)} %copy-done.5, bf16[8,10,3,2,16,128]{5,4,3,2,1,0:T(8,128)(2,1)} %bitcast.99, pred[8,10]{1,0:T(8,128)(4,1)S(1)} %copy-done.6, bf16[8,10]{1,0:T(8,128)(2,1)S(1)} %fusion.29), kind=kOutput, calls=%fused_computation.8.clone.1 | convolution fusion | flops 513146880 | bytes 18481472 | tf_op jit(solution)/shard_map/while/body/eval_jaxpr/fsarkt,frktc->rfsac/dot_general | solution.py:75
  324.7 6.7 %collective-permute-start = (bf16[3,2,16,1024]{3,2,1,0:T(8,128)(2,1)S(1)}, bf16[3,2,16,1024]{3,2,1,0:T(8,128)(2,1)S(1)}, u32[]{:S(2)}, u32[]{:S(2)}) collective-permute-start(bf16[3,2,16,1024]{3,2,1,0:T(8,128)(2,1)S(1)} %get-tuple-element.365), channel_id=1, source_target_pairs={{2,0},{4,2},{6,4},{8,6},{10,8},{12,10},{14,12},{16,14},{18,16},{20... | collective-permute-start | bytes 589832 | tf_op jit(solution)/shard_map/while/body/eval_jaxpr/ppermute | solution.py:19
  337.7 8.2 %gather_fusion = bf16[80,3,128,256]{3,2,1,0:T(8,128)(2,1)} fusion(bf16[3,8,128,256]{3,2,1,0:T(8,128)(2,1)S(1)} %dynamic-slice_bitcast_fusion.2, s32[1024]{0:T(1024)S(1)} %pad_clamp_fusion.4), kind=kCustom, calls=%fused_computation.1.clone.1 | custom fusion | bytes 31457600 | tf_op jit(solution)/shard_map/while/body/eval_jaxpr/jit(_take)/gather | solution.py:74
  350.0 8.0 %fusion.30 = f32[8,3,2,16,256]{4,3,2,1,0:T(8,128)S(1)} fusion(bf16[8,10,3,128,256]{4,3,2,1,0:T(8,128)(2,1)} %bitcast.98, pred[8,10]{1,0:T(8,128)(4,1)S(1)} %copy-done.5, bf16[8,10,3,2,16,128]{5,4,3,2,1,0:T(8,128)(2,1)} %bitcast.99, pred[8,10]{1,0:T(8,128)(4,1)S(1)} %copy-done.6, bf16[8,10]{1,0:T(8,128)(2,1)S(1)} %fusion.29), kind=kOutput, calls=%fused_computation.8.clone.1 | convolution fusion | flops 513146880 | bytes 18481472 | tf_op jit(solution)/shard_map/while/body/eval_jaxpr/fsarkt,frktc->rfsac/dot_general | solution.py:75
  359.8 6.7 %collective-permute-start = (bf16[3,2,16,1024]{3,2,1,0:T(8,128)(2,1)S(1)}, bf16[3,2,16,1024]{3,2,1,0:T(8,128)(2,1)S(1)}, u32[]{:S(2)}, u32[]{:S(2)}) collective-permute-start(bf16[3,2,16,1024]{3,2,1,0:T(8,128)(2,1)S(1)} %get-tuple-element.365), channel_id=1, source_target_pairs={{2,0},{4,2},{6,4},{8,6},{10,8},{12,10},{14,12},{16,14},{18,16},{20... | collective-permute-start | bytes 589832 | tf_op jit(solution)/shard_map/while/body/eval_jaxpr/ppermute | solution.py:19
  372.8 8.1 %gather_fusion = bf16[80,3,128,256]{3,2,1,0:T(8,128)(2,1)} fusion(bf16[3,8,128,256]{3,2,1,0:T(8,128)(2,1)S(1)} %dynamic-slice_bitcast_fusion.2, s32[1024]{0:T(1024)S(1)} %pad_clamp_fusion.4), kind=kCustom, calls=%fused_computation.1.clone.1 | custom fusion | bytes 31457600 | tf_op jit(solution)/shard_map/while/body/eval_jaxpr/jit(_take)/gather | solution.py:74
  382.7 2.4 gather_fusion.1
  385.1 8.0 %fusion.30 = f32[8,3,2,16,256]{4,3,2,1,0:T(8,128)S(1)} fusion(bf16[8,10,3,128,256]{4,3,2,1,0:T(8,128)(2,1)} %bitcast.98, pred[8,10]{1,0:T(8,128)(4,1)S(1)} %copy-done.5, bf16[8,10,3,2,16,128]{5,4,3,2,1,0:T(8,128)(2,1)} %bitcast.99, pred[8,10]{1,0:T(8,128)(4,1)S(1)} %copy-done.6, bf16[8,10]{1,0:T(8,128)(2,1)S(1)} %fusion.29), kind=kOutput, calls=%fused_computation.8.clone.1 | convolution fusion | flops 513146880 | bytes 18481472 | tf_op jit(solution)/shard_map/while/body/eval_jaxpr/fsarkt,frktc->rfsac/dot_general | solution.py:75
  394.9 6.7 %collective-permute-start = (bf16[3,2,16,1024]{3,2,1,0:T(8,128)(2,1)S(1)}, bf16[3,2,16,1024]{3,2,1,0:T(8,128)(2,1)S(1)}, u32[]{:S(2)}, u32[]{:S(2)}) collective-permute-start(bf16[3,2,16,1024]{3,2,1,0:T(8,128)(2,1)S(1)} %get-tuple-element.365), channel_id=1, source_target_pairs={{2,0},{4,2},{6,4},{8,6},{10,8},{12,10},{14,12},{16,14},{18,16},{20... | collective-permute-start | bytes 589832 | tf_op jit(solution)/shard_map/while/body/eval_jaxpr/ppermute | solution.py:19
  407.9 8.2 %gather_fusion = bf16[80,3,128,256]{3,2,1,0:T(8,128)(2,1)} fusion(bf16[3,8,128,256]{3,2,1,0:T(8,128)(2,1)S(1)} %dynamic-slice_bitcast_fusion.2, s32[1024]{0:T(1024)S(1)} %pad_clamp_fusion.4), kind=kCustom, calls=%fused_computation.1.clone.1 | custom fusion | bytes 31457600 | tf_op jit(solution)/shard_map/while/body/eval_jaxpr/jit(_take)/gather | solution.py:74
  420.3 8.0 %fusion.30 = f32[8,3,2,16,256]{4,3,2,1,0:T(8,128)S(1)} fusion(bf16[8,10,3,128,256]{4,3,2,1,0:T(8,128)(2,1)} %bitcast.98, pred[8,10]{1,0:T(8,128)(4,1)S(1)} %copy-done.5, bf16[8,10,3,2,16,128]{5,4,3,2,1,0:T(8,128)(2,1)} %bitcast.99, pred[8,10]{1,0:T(8,128)(4,1)S(1)} %copy-done.6, bf16[8,10]{1,0:T(8,128)(2,1)S(1)} %fusion.29), kind=kOutput, calls=%fused_computation.8.clone.1 | convolution fusion | flops 513146880 | bytes 18481472 | tf_op jit(solution)/shard_map/while/body/eval_jaxpr/fsarkt,frktc->rfsac/dot_general | solution.py:75
  430.8 9.8 %all_to_all.10 = f32[8,1,1024]{2,1,0:T(1,128)S(1)} all-to-all(f32[8,1,1024]{2,1,0:T(1,128)S(1)} %reshape.218), channel_id=1, replica_groups=mesh['depth'=8,'lat'=32,'freq'=2] {'depth'}, dimensions={0} | all-to-all | bytes 65536 | tf_op jit(solution)/shard_map/all_to_all | solution.py:58
  440.7 8.4 %psum.7 = f32[1024]{0:T(1024)S(1)} all-reduce(f32[1024]{0:T(1024)S(1)} %reduce_sum.20), channel_id=1, replica_groups=mesh['depth'=8,'lat'=32,'freq'=2] {'freq'}, use_global_device_ids=true, to_apply=%region_4.5 | all-reduce | flops 1024 | bytes 8192 | tf_op jit(solution)/shard_map/psum | solution.py:119
  (263 shorter events, 98.5 us)
Async XLA Ops:
  6.5 29.7 %copy-start = (bf16[3,2,128,1024]{3,2,1,0:T(8,128)(2,1)S(1)}, bf16[3,2,128,1024]{3,2,1,0:T(8,128)(2,1)}, u32[]{:S(2)}) copy-start(bf16[3,2,128,1024]{3,2,1,0:T(8,128)(2,1)} %param.8) | copy-start | bytes 4718596
  6.5 141.4 %all-gather.2.cloned.1.call-start = ((), (), s32[]{:S(2)}) async-start(), calls=%async_computation.2 | async-start | bytes 14155776 | tf_op jit(solution)/shard_map/all_gather | solution.py:97
  8.6 28.5 %all-to-all-start = ((f32[8,1,1024]{2,1,0:T(1,128)}), f32[8,1,1024]{2,1,0:T(1,128)S(1)}, u32[]{:S(2)}, u32[]{:S(2)}) async-start(f32[8,1,1024]{2,1,0:T(1,128)} %broadcast_in_dim.88), calls=%async_computation | async-start | bytes 65536 | tf_op jit(solution)/shard_map/all_to_all | solution.py:37
  148.0 10.5 %copy-start.1 = (s32[8,8,10]{2,1,0:T(8,128)}, s32[8,8,10]{2,1,0:T(8,128)S(1)}, u32[]{:S(2)}) copy-start(s32[8,8,10]{2,1,0:T(8,128)S(1)} %get-tuple-element.381) | copy-start | bytes 7684 | tf_op jit(solution)/shard_map/while
  148.0 10.5 %copy-start.3 = (s32[8,8,10]{2,1,0:T(8,128)}, s32[8,8,10]{2,1,0:T(8,128)S(1)}, u32[]{:S(2)}) copy-start(s32[8,8,10]{2,1,0:T(8,128)S(1)} %get-tuple-element.378) | copy-start | bytes 7684 | tf_op jit(solution)/shard_map/while
  148.0 23.0 %collective-permute-start = (bf16[3,2,16,1024]{3,2,1,0:T(8,128)(2,1)S(1)}, bf16[3,2,16,1024]{3,2,1,0:T(8,128)(2,1)S(1)}, u32[]{:S(2)}, u32[]{:S(2)}) collective-permute-start(bf16[3,2,16,1024]{3,2,1,0:T(8,128)(2,1)S(1)} %get-tuple-element.365), channel_id=1, source_target_pairs={{2,0},{4,2},{6,4},{8,6},{10,8},{12,10},{14,12},{16,14},{18,16},{20... | collective-permute-start | bytes 589832 | tf_op jit(solution)/shard_map/while/body/eval_jaxpr/ppermute | solution.py:19
  155.8 15.2 %collective-permute-start.1 = (bf16[3,2,16,1024]{3,2,1,0:T(8,128)(2,1)S(1)}, bf16[3,2,16,1024]{3,2,1,0:T(8,128)(2,1)}, u32[]{:S(2)}, u32[]{:S(2)}) collective-permute-start(bf16[3,2,16,1024]{3,2,1,0:T(8,128)(2,1)S(1)} %get-tuple-element.365), channel_id=1, source_target_pairs={{0,2},{2,4},{4,6},{6,8},{8,10},{10,12},{12,14},{14,16},{16,18},{18... | collective-permute-start | bytes 589832 | tf_op jit(solution)/shard_map/while/body/eval_jaxpr/ppermute | solution.py:16
  184.2 9.4 %copy-start.1 = (s32[8,8,10]{2,1,0:T(8,128)}, s32[8,8,10]{2,1,0:T(8,128)S(1)}, u32[]{:S(2)}) copy-start(s32[8,8,10]{2,1,0:T(8,128)S(1)} %get-tuple-element.381) | copy-start | bytes 7684 | tf_op jit(solution)/shard_map/while
  184.2 9.4 %copy-start.3 = (s32[8,8,10]{2,1,0:T(8,128)}, s32[8,8,10]{2,1,0:T(8,128)S(1)}, u32[]{:S(2)}) copy-start(s32[8,8,10]{2,1,0:T(8,128)S(1)} %get-tuple-element.378) | copy-start | bytes 7684 | tf_op jit(solution)/shard_map/while
  184.2 21.9 %collective-permute-start = (bf16[3,2,16,1024]{3,2,1,0:T(8,128)(2,1)S(1)}, bf16[3,2,16,1024]{3,2,1,0:T(8,128)(2,1)S(1)}, u32[]{:S(2)}, u32[]{:S(2)}) collective-permute-start(bf16[3,2,16,1024]{3,2,1,0:T(8,128)(2,1)S(1)} %get-tuple-element.365), channel_id=1, source_target_pairs={{2,0},{4,2},{6,4},{8,6},{10,8},{12,10},{14,12},{16,14},{18,16},{20... | collective-permute-start | bytes 589832 | tf_op jit(solution)/shard_map/while/body/eval_jaxpr/ppermute | solution.py:19
  191.0 15.2 %collective-permute-start.1 = (bf16[3,2,16,1024]{3,2,1,0:T(8,128)(2,1)S(1)}, bf16[3,2,16,1024]{3,2,1,0:T(8,128)(2,1)}, u32[]{:S(2)}, u32[]{:S(2)}) collective-permute-start(bf16[3,2,16,1024]{3,2,1,0:T(8,128)(2,1)S(1)} %get-tuple-element.365), channel_id=1, source_target_pairs={{0,2},{2,4},{4,6},{6,8},{8,10},{10,12},{12,14},{14,16},{16,18},{18... | collective-permute-start | bytes 589832 | tf_op jit(solution)/shard_map/while/body/eval_jaxpr/ppermute | solution.py:16
  219.4 9.3 %copy-start.3 = (s32[8,8,10]{2,1,0:T(8,128)}, s32[8,8,10]{2,1,0:T(8,128)S(1)}, u32[]{:S(2)}) copy-start(s32[8,8,10]{2,1,0:T(8,128)S(1)} %get-tuple-element.378) | copy-start | bytes 7684 | tf_op jit(solution)/shard_map/while
  219.4 21.8 %collective-permute-start = (bf16[3,2,16,1024]{3,2,1,0:T(8,128)(2,1)S(1)}, bf16[3,2,16,1024]{3,2,1,0:T(8,128)(2,1)S(1)}, u32[]{:S(2)}, u32[]{:S(2)}) collective-permute-start(bf16[3,2,16,1024]{3,2,1,0:T(8,128)(2,1)S(1)} %get-tuple-element.365), channel_id=1, source_target_pairs={{2,0},{4,2},{6,4},{8,6},{10,8},{12,10},{14,12},{16,14},{18,16},{20... | collective-permute-start | bytes 589832 | tf_op jit(solution)/shard_map/while/body/eval_jaxpr/ppermute | solution.py:19
  226.0 15.2 %collective-permute-start.1 = (bf16[3,2,16,1024]{3,2,1,0:T(8,128)(2,1)S(1)}, bf16[3,2,16,1024]{3,2,1,0:T(8,128)(2,1)}, u32[]{:S(2)}, u32[]{:S(2)}) collective-permute-start(bf16[3,2,16,1024]{3,2,1,0:T(8,128)(2,1)S(1)} %get-tuple-element.365), channel_id=1, source_target_pairs={{0,2},{2,4},{4,6},{6,8},{8,10},{10,12},{12,14},{14,16},{16,18},{18... | collective-permute-start | bytes 589832 | tf_op jit(solution)/shard_map/while/body/eval_jaxpr/ppermute | solution.py:16
  254.5 9.4 %copy-start.1 = (s32[8,8,10]{2,1,0:T(8,128)}, s32[8,8,10]{2,1,0:T(8,128)S(1)}, u32[]{:S(2)}) copy-start(s32[8,8,10]{2,1,0:T(8,128)S(1)} %get-tuple-element.381) | copy-start | bytes 7684 | tf_op jit(solution)/shard_map/while
  254.5 9.4 %copy-start.3 = (s32[8,8,10]{2,1,0:T(8,128)}, s32[8,8,10]{2,1,0:T(8,128)S(1)}, u32[]{:S(2)}) copy-start(s32[8,8,10]{2,1,0:T(8,128)S(1)} %get-tuple-element.378) | copy-start | bytes 7684 | tf_op jit(solution)/shard_map/while
  254.5 21.9 %collective-permute-start = (bf16[3,2,16,1024]{3,2,1,0:T(8,128)(2,1)S(1)}, bf16[3,2,16,1024]{3,2,1,0:T(8,128)(2,1)S(1)}, u32[]{:S(2)}, u32[]{:S(2)}) collective-permute-start(bf16[3,2,16,1024]{3,2,1,0:T(8,128)(2,1)S(1)} %get-tuple-element.365), channel_id=1, source_target_pairs={{2,0},{4,2},{6,4},{8,6},{10,8},{12,10},{14,12},{16,14},{18,16},{20... | collective-permute-start | bytes 589832 | tf_op jit(solution)/shard_map/while/body/eval_jaxpr/ppermute | solution.py:19
  261.2 15.2 %collective-permute-start.1 = (bf16[3,2,16,1024]{3,2,1,0:T(8,128)(2,1)S(1)}, bf16[3,2,16,1024]{3,2,1,0:T(8,128)(2,1)}, u32[]{:S(2)}, u32[]{:S(2)}) collective-permute-start(bf16[3,2,16,1024]{3,2,1,0:T(8,128)(2,1)S(1)} %get-tuple-element.365), channel_id=1, source_target_pairs={{0,2},{2,4},{4,6},{6,8},{8,10},{10,12},{12,14},{14,16},{16,18},{18... | collective-permute-start | bytes 589832 | tf_op jit(solution)/shard_map/while/body/eval_jaxpr/ppermute | solution.py:16
  289.6 9.3 %copy-start.1 = (s32[8,8,10]{2,1,0:T(8,128)}, s32[8,8,10]{2,1,0:T(8,128)S(1)}, u32[]{:S(2)}) copy-start(s32[8,8,10]{2,1,0:T(8,128)S(1)} %get-tuple-element.381) | copy-start | bytes 7684 | tf_op jit(solution)/shard_map/while
  289.6 9.4 %copy-start.3 = (s32[8,8,10]{2,1,0:T(8,128)}, s32[8,8,10]{2,1,0:T(8,128)S(1)}, u32[]{:S(2)}) copy-start(s32[8,8,10]{2,1,0:T(8,128)S(1)} %get-tuple-element.378) | copy-start | bytes 7684 | tf_op jit(solution)/shard_map/while
  289.6 21.9 %collective-permute-start = (bf16[3,2,16,1024]{3,2,1,0:T(8,128)(2,1)S(1)}, bf16[3,2,16,1024]{3,2,1,0:T(8,128)(2,1)S(1)}, u32[]{:S(2)}, u32[]{:S(2)}) collective-permute-start(bf16[3,2,16,1024]{3,2,1,0:T(8,128)(2,1)S(1)} %get-tuple-element.365), channel_id=1, source_target_pairs={{2,0},{4,2},{6,4},{8,6},{10,8},{12,10},{14,12},{16,14},{18,16},{20... | collective-permute-start | bytes 589832 | tf_op jit(solution)/shard_map/while/body/eval_jaxpr/ppermute | solution.py:19
  296.3 15.2 %collective-permute-start.1 = (bf16[3,2,16,1024]{3,2,1,0:T(8,128)(2,1)S(1)}, bf16[3,2,16,1024]{3,2,1,0:T(8,128)(2,1)}, u32[]{:S(2)}, u32[]{:S(2)}) collective-permute-start(bf16[3,2,16,1024]{3,2,1,0:T(8,128)(2,1)S(1)} %get-tuple-element.365), channel_id=1, source_target_pairs={{0,2},{2,4},{4,6},{6,8},{8,10},{10,12},{12,14},{14,16},{16,18},{18... | collective-permute-start | bytes 589832 | tf_op jit(solution)/shard_map/while/body/eval_jaxpr/ppermute | solution.py:16
  324.7 21.8 %collective-permute-start = (bf16[3,2,16,1024]{3,2,1,0:T(8,128)(2,1)S(1)}, bf16[3,2,16,1024]{3,2,1,0:T(8,128)(2,1)S(1)}, u32[]{:S(2)}, u32[]{:S(2)}) collective-permute-start(bf16[3,2,16,1024]{3,2,1,0:T(8,128)(2,1)S(1)} %get-tuple-element.365), channel_id=1, source_target_pairs={{2,0},{4,2},{6,4},{8,6},{10,8},{12,10},{14,12},{16,14},{18,16},{20... | collective-permute-start | bytes 589832 | tf_op jit(solution)/shard_map/while/body/eval_jaxpr/ppermute | solution.py:19
  331.4 15.2 %collective-permute-start.1 = (bf16[3,2,16,1024]{3,2,1,0:T(8,128)(2,1)S(1)}, bf16[3,2,16,1024]{3,2,1,0:T(8,128)(2,1)}, u32[]{:S(2)}, u32[]{:S(2)}) collective-permute-start(bf16[3,2,16,1024]{3,2,1,0:T(8,128)(2,1)S(1)} %get-tuple-element.365), channel_id=1, source_target_pairs={{0,2},{2,4},{4,6},{6,8},{8,10},{10,12},{12,14},{14,16},{16,18},{18... | collective-permute-start | bytes 589832 | tf_op jit(solution)/shard_map/while/body/eval_jaxpr/ppermute | solution.py:16
  359.8 9.4 %copy-start.1 = (s32[8,8,10]{2,1,0:T(8,128)}, s32[8,8,10]{2,1,0:T(8,128)S(1)}, u32[]{:S(2)}) copy-start(s32[8,8,10]{2,1,0:T(8,128)S(1)} %get-tuple-element.381) | copy-start | bytes 7684 | tf_op jit(solution)/shard_map/while
  359.8 9.4 %copy-start.3 = (s32[8,8,10]{2,1,0:T(8,128)}, s32[8,8,10]{2,1,0:T(8,128)S(1)}, u32[]{:S(2)}) copy-start(s32[8,8,10]{2,1,0:T(8,128)S(1)} %get-tuple-element.378) | copy-start | bytes 7684 | tf_op jit(solution)/shard_map/while
  359.8 21.8 %collective-permute-start = (bf16[3,2,16,1024]{3,2,1,0:T(8,128)(2,1)S(1)}, bf16[3,2,16,1024]{3,2,1,0:T(8,128)(2,1)S(1)}, u32[]{:S(2)}, u32[]{:S(2)}) collective-permute-start(bf16[3,2,16,1024]{3,2,1,0:T(8,128)(2,1)S(1)} %get-tuple-element.365), channel_id=1, source_target_pairs={{2,0},{4,2},{6,4},{8,6},{10,8},{12,10},{14,12},{16,14},{18,16},{20... | collective-permute-start | bytes 589832 | tf_op jit(solution)/shard_map/while/body/eval_jaxpr/ppermute | solution.py:19
  366.5 15.1 %collective-permute-start.1 = (bf16[3,2,16,1024]{3,2,1,0:T(8,128)(2,1)S(1)}, bf16[3,2,16,1024]{3,2,1,0:T(8,128)(2,1)}, u32[]{:S(2)}, u32[]{:S(2)}) collective-permute-start(bf16[3,2,16,1024]{3,2,1,0:T(8,128)(2,1)S(1)} %get-tuple-element.365), channel_id=1, source_target_pairs={{0,2},{2,4},{4,6},{6,8},{8,10},{10,12},{12,14},{14,16},{16,18},{18... | collective-permute-start | bytes 589832 | tf_op jit(solution)/shard_map/while/body/eval_jaxpr/ppermute | solution.py:16
  394.9 9.4 %copy-start.1 = (s32[8,8,10]{2,1,0:T(8,128)}, s32[8,8,10]{2,1,0:T(8,128)S(1)}, u32[]{:S(2)}) copy-start(s32[8,8,10]{2,1,0:T(8,128)S(1)} %get-tuple-element.381) | copy-start | bytes 7684 | tf_op jit(solution)/shard_map/while
  394.9 9.4 %copy-start.3 = (s32[8,8,10]{2,1,0:T(8,128)}, s32[8,8,10]{2,1,0:T(8,128)S(1)}, u32[]{:S(2)}) copy-start(s32[8,8,10]{2,1,0:T(8,128)S(1)} %get-tuple-element.378) | copy-start | bytes 7684 | tf_op jit(solution)/shard_map/while
  394.9 21.9 %collective-permute-start = (bf16[3,2,16,1024]{3,2,1,0:T(8,128)(2,1)S(1)}, bf16[3,2,16,1024]{3,2,1,0:T(8,128)(2,1)S(1)}, u32[]{:S(2)}, u32[]{:S(2)}) collective-permute-start(bf16[3,2,16,1024]{3,2,1,0:T(8,128)(2,1)S(1)} %get-tuple-element.365), channel_id=1, source_target_pairs={{2,0},{4,2},{6,4},{8,6},{10,8},{12,10},{14,12},{16,14},{18,16},{20... | collective-permute-start | bytes 589832 | tf_op jit(solution)/shard_map/while/body/eval_jaxpr/ppermute | solution.py:19
  401.6 15.2 %collective-permute-start.1 = (bf16[3,2,16,1024]{3,2,1,0:T(8,128)(2,1)S(1)}, bf16[3,2,16,1024]{3,2,1,0:T(8,128)(2,1)}, u32[]{:S(2)}, u32[]{:S(2)}) collective-permute-start(bf16[3,2,16,1024]{3,2,1,0:T(8,128)(2,1)S(1)} %get-tuple-element.365), channel_id=1, source_target_pairs={{0,2},{2,4},{4,6},{6,8},{8,10},{10,12},{12,14},{14,16},{16,18},{18... | collective-permute-start | bytes 589832 | tf_op jit(solution)/shard_map/while/body/eval_jaxpr/ppermute | solution.py:16
  (35 other events, 94.4 us)
Sparse Core Ops, SparseCore 0:
  9.4 138.4 all-gather.1
where the time goes:
time: 463 us; the launch traced here: 457 us
  local copies, waits for them, and re-layouts  114 us (25%)
  waiting for transfers between devices  111 us (24%)
  starting transfers between devices  76.4 us (17%)
  matrix products  64.4 us (14%)
  other arithmetic  38.8 us (8%)
  blocking collectives  38.1 us (8%)
  between operations  13.4 us (3%)
    all_gather x1, waiting for transfers between devices, per_device(): pool_all = lax.all_gather(pool, 'depth', axis=0, tiled=True)  110 us
    gather x8, local copies, waits for them, and re-layouts, extrapolate(): chosen = jnp.take(pool_level, block_level, axis=1)  65.3 us
    dot_general x8, matrix products, extrapolate(): jnp.einsum('fsarkt,frktc->rfsac', picked, chosen, preferred_element_type=...  64.4 us
    ppermute x8, starting transfers between devices, extended_2(): lax.ppermute(lax.slice_in_dim(block, 0, width, axis=dim), axis, backward)  54.7 us
    all_gather x1, blocking collectives, in_one_piece(): lax.all_gather(both, axis, axis=dim, tiled=True)  19.8 us
    gather x8, local copies, waits for them, and re-layouts, extrapolate(): jnp.take(tile_grid, local_ids, axis=3)  19.3 us
    ppermute x8, starting transfers between devices, extended_2(): lax.ppermute(lax.slice_in_dim(block, block.shape[dim] - width, None, axis...  15.4 us
    squeeze x8, local copies, waits for them, and re-layouts, level_step(): lax.dynamic_index_in_dim(pool_all, level_index, 0, keepdims=False)  12.1 us
  transfers between devices with their start and end apart: 18, of which 1 were waited for; matrix products, arithmetic and copies ran while one was open for 24% of the time, Pallas kernels for 0%

commit v1 on v0

v1 whole, which is shorter than its diff:
```python
import jax
import jax.numpy as jnp
from jax import lax
from jax.experimental import pallas as pl
from jax.experimental.pallas import tpu as pltpu
from jax.sharding import PartitionSpec as P

MESH = pl.DeviceIdType.MESH
ANY = pl.BlockSpec(memory_space=pl.ANY)
BF = jnp.bfloat16
F32 = jnp.float32
DEAD = 8 * 1024


def place():
    d = lax.axis_index("depth")
    a = lax.axis_index("lat")
    c = lax.axis_index("freq")
    return d, a // 4, a % 4, c


def remote(src, dst, send, recv, d, z, x, c):
    return pltpu.make_async_remote_copy(
        src_ref=src,
        dst_ref=dst,
        send_sem=send,
        recv_sem=recv,
        device_id=(d, z * 4 + x, c),
        device_id_type=MESH,
    )


def spread_kernel(
    wsrc, fac, ints, pool, wave, fac_all, ints_all, pool_all,
    w_send, w_recv, y_send, y_recv, x_send, x_recv, z_send, z_recv, s_send, s_recv,
    p_send, p_recv, q_send, q_recv, l_sem,
):
    d, z, x, c = place()
    a = z * 4 + x
    other = 1 - c
    active = z < 6
    own_core = z // 3
    half = pl.ds(4 * c, 4)

    mine = pool.at[0, z % 3]
    here = pltpu.make_async_copy(mine, pool_all.at[d], l_sem.at[0])
    over = remote(mine, pool_all.at[d], q_send.at[7], q_recv.at[7], d, z, x, other)
    gives = jnp.logical_and(active, c == own_core)
    takes = jnp.logical_and(active, c != own_core)

    @pl.when(gives)
    def _():
        over.start()
        here.start()

    near = d // 4 == c
    fac_here = pltpu.make_async_copy(fac, fac_all.at[d, z, x], l_sem.at[1])
    ints_here = pltpu.make_async_copy(ints, ints_all.at[d, z, x], l_sem.at[2])

    def y_copies(step):
        to = (d + step) % 8
        return (
            remote(fac, fac_all.at[d, z, x], y_send.at[0, step], y_recv.at[0, d % 4], to, z, x, c),
            remote(ints, ints_all.at[d, z, x], y_send.at[1, step], y_recv.at[1, d % 4], to, z, x, c),
        )

    @pl.when(near)
    def _():
        fac_here.start()
        ints_here.start()
        for step in range(1, 8):
            for copy in y_copies(step):
                copy.start()

    def w_copy(i):
        part, u = i // 8, i % 8
        return (
            wsrc.at[part, u], 3 * c + part, u // 2, u % 2
        )

    def w_self(tz, tx, tc):
        return jnp.logical_and(tz * 4 + tx == a, tc == c)

    @pl.loop(0, 24)
    def _(i):
        src, tz, tx, tc = w_copy(i)
        same = w_self(tz, tx, tc)

        @pl.when(same)
        def _():
            pltpu.make_async_copy(src, wave.at[a], l_sem.at[3]).start()

        @pl.when(jnp.logical_not(same))
        def _():
            remote(src, wave.at[a], w_send.at[i], w_recv.at[a], d, tz, tx, tc).start()

    @pl.when(near)
    def _():
        fac_here.wait()
        ints_here.wait()

    for k in range(4):
        level = 4 * c + k

        @pl.when(level != d)
        def _():
            for kind, whole in ((0, fac_all), (1, ints_all)):
                pltpu.make_async_copy(
                    whole.at[level, z, x], whole.at[level, z, x], y_recv.at[kind, k]
                ).wait()

    def x_copies(step):
        to = (x + step) % 4
        return [
            remote(whole.at[half, z, x], whole.at[half, z, x], x_send.at[kind, step],
                   x_recv.at[kind, step], d, z, to, c)
            for kind, whole in ((0, fac_all), (1, ints_all))
        ]

    for step in range(1, 4):
        for copy in x_copies(step):
            copy.start()

    @pl.when(gives)
    def _():
        here.wait()

    @pl.when(takes)
    def _():
        over.wait_recv()

    def ring_copy(way, step):
        if way == 0:
            level, to = (d - step + 8) % 8, (d + 1) % 8
        else:
            level, to = (d + step) % 8, (d + 7) % 8
        at = pool_all.at[level, half]
        return remote(at, at, p_send.at[way, step], p_recv.at[way, step], to, z, x, c)

    def share(way, step):
        level = (d - 1 - step + 8) % 8 if way == 0 else (d + 1 + step) % 8
        at = pool_all.at[level, half]
        i = step if way == 0 else 4 + step
        return remote(at, at, q_send.at[i], q_recv.at[i], d, z, x, other)

    @pl.when(active)
    def _():
        ring_copy(0, 0).start()
        ring_copy(1, 0).start()

    for step in range(1, 4):
        for copy in x_copies(step):
            copy.wait_recv()

    def z_copies(step):
        to = (z + step) % 8
        return to, [
            remote(whole.at[half, z], whole.at[half, z], z_send.at[kind, step],
                   z_recv.at[kind, step], d, to, x, c)
            for kind, whole in ((0, fac_all), (1, ints_all))
        ]

    for step in range(1, 8):
        to, copies = z_copies(step)

        @pl.when(to < 6)
        def _():
            for copy in copies:
                copy.start()

    @pl.when(active)
    def _():
        for step in range(4):
            ring_copy(0, step).wait_recv()
            if step < 3:
                ring_copy(0, step + 1).start()
            share(0, step).start()
            if step < 3:
                ring_copy(1, step).wait_recv()
                if step < 2:
                    ring_copy(1, step + 1).start()
                share(1, step).start()

        for step in range(1, 8):
            for copy in z_copies(step)[1]:
                copy.wait_recv()
        swaps = [
            remote(whole.at[half], whole.at[half], s_send.at[kind], s_recv.at[kind], d, z, x, other)
            for kind, whole in ((0, fac_all), (1, ints_all))
        ]
        for copy in swaps:
            copy.start()
        for copy in swaps:
            copy.wait()
        for way, step in ((0, 0), (0, 1), (0, 2), (0, 3), (1, 0), (1, 1), (1, 2)):
            ring_copy(way, step).wait_send()
            share(way, step).wait()

        @pl.loop(0, 32)
        def _(i):
            same = jnp.logical_and(i == a, c == own_core)

            @pl.when(same)
            def _():
                pltpu.make_async_copy(wave.at[i], wave.at[i], l_sem.at[3]).wait()

            @pl.when(jnp.logical_not(same))
            def _():
                pltpu.make_async_copy(wave.at[i], wave.at[i], w_recv.at[i]).wait()

    @pl.when(gives)
    def _():
        over.wait_send()

    @pl.when(near)
    def _():
        for step in range(1, 8):
            for copy in y_copies(step):
                copy.wait_send()

    for step in range(1, 4):
        for copy in x_copies(step):
            copy.wait_send()
    for step in range(1, 8):
        to, copies = z_copies(step)

        @pl.when(to < 6)
        def _():
            for copy in copies:
                copy.wait_send()

    @pl.loop(0, 24)
    def _(i):
        src, tz, tx, tc = w_copy(i)

        @pl.when(jnp.logical_not(w_self(tz, tx, tc)))
        def _():
            remote(src, wave.at[a], w_send.at[i], w_recv.at[a], d, tz, tx, tc).wait_send()


def spread(wsrc, fac, ints, pool):
    dma = pltpu.SemaphoreType.DMA
    return pl.pallas_call(
        spread_kernel,
        out_shape=(
            jax.ShapeDtypeStruct((32, 32, 128), BF),
            jax.ShapeDtypeStruct((8, 8, 4, 8, 128), F32),
            jax.ShapeDtypeStruct((8, 8, 4, 1, 128), jnp.int32),
            jax.ShapeDtypeStruct((8, 8, 128, 256), BF),
        ),
        in_specs=[ANY] * 4,
        out_specs=(ANY,) * 4,
        scratch_shapes=[
            dma((24,)), dma((32,)),
            dma((2, 8)), dma((2, 4)), dma((2, 4)), dma((2, 4)), dma((2, 8)), dma((2, 8)),
            dma((2,)), dma((2,)),
            dma((2, 4)), dma((2, 4)), dma((8,)), dma((8,)), dma((4,)),
        ],
        compiler_params=pltpu.CompilerParams(has_side_effects=True),
        name="spread",
    )(wsrc, fac, ints, pool)


def levels_kernel(ints, wave, fac, pool, image, field, prod, rows):
    level = pl.program_id(0)
    _, z, _, _ = place()

    @pl.when(z < 6)
    def _():
        @pl.when(level == 0)
        def _():
            prod[DEAD : DEAD + 8, :] = jnp.zeros((8, 128), F32)

            @pl.loop(0, 16)
            def _(i):
                pair = [wave[2 * i + k].astype(F32) for k in range(2)]
                at = pl.ds(pl.multiple_of(16 * i, 16), 16)
                put_field(
                    field, at,
                    [jnp.concatenate([p[8 * q : 8 * q + 8] for p in pair], 0) for q in range(4)],
                )

        for pair in range(4):
            b0, b1 = pool[0, 2 * pair], pool[0, 2 * pair + 1]
            weights = jnp.concatenate(
                [
                    jnp.concatenate([b0[:, :128], b1[:, :128]], 1),
                    jnp.concatenate([b0[:, 128:], b1[:, 128:]], 1),
                ],
                0,
            )
            for q in range(4):
                out = jnp.dot(field[q], weights, preferred_element_type=F32)
                for k in range(2):
                    base = (2 * pair + k) * 1024 + q
                    prod[pl.ds(base, 256, stride=4), :] = out[:, 128 * k : 128 * k + 128]

        @pl.loop(0, 32)
        def _(g):
            most = ints[level, g, 80]

            def slot(k, sums):
                return tuple(
                    sums[r] + prod[pl.ds(ints[level, g, k * 8 + r], 4), :] for r in range(8)
                )

            sums = lax.fori_loop(0, most, slot, tuple(jnp.zeros((4, 128), F32) for _ in range(8)))
            for r in range(8):
                rows[pl.ds(pl.multiple_of(g * 32, 32) + 4 * r, 4), :] = sums[r]

        @pl.loop(0, 16)
        def _(i):
            at = pl.ds(pl.multiple_of(16 * i, 16), 16)
            scale = fac[0, at, :]
            new = [rows[pl.ds(64 * i + q, 16, stride=4), :] * scale for q in range(4)]
            image[0, at, :] = (new[0] * new[0] + new[1] * new[1]) + (
                new[2] * new[2] + new[3] * new[3]
            )
            put_field(field, at, new)


def put_field(field, at, parts):
    for s in range(2):
        re, im = parts[2 * s].astype(BF), parts[2 * s + 1].astype(BF)
        field[2 * s, at, :128] = re
        field[2 * s, at, 128:] = -im
        field[2 * s + 1, at, :128] = im
        field[2 * s + 1, at, 128:] = re


def levels(ints, wave, fac, pool):
    return pl.pallas_call(
        levels_kernel,
        grid=(8,),
        out_shape=jax.ShapeDtypeStruct((8, 256, 128), F32),
        in_specs=[
            pl.BlockSpec(memory_space=pltpu.SMEM),
            pl.BlockSpec((32, 32, 128), lambda i: (0, 0, 0)),
            pl.BlockSpec((1, 256, 128), lambda i: (i, 0, 0)),
            pl.BlockSpec((1, 8, 128, 256), lambda i: (i, 0, 0, 0)),
        ],
        out_specs=pl.BlockSpec((1, 256, 128), lambda i: (i, 0, 0)),
        scratch_shapes=[
            pltpu.VMEM((4, 256, 256), BF),
            pltpu.VMEM((DEAD + 8, 128), F32),
            pltpu.VMEM((1024, 128), F32),
        ],
        compiler_params=pltpu.CompilerParams(vmem_limit_bytes=40 * 2**20),
        name="levels",
    )(ints, wave, fac, pool)


def collect_kernel(
    part, out, got, in_sib, half_sum, in_x, x_sum, in_y, y_sum, in_z, done,
    l_sem, s_send, s_recv, x_send, x_recv, y_send, y_recv, z_send, z_recv, e_send, e_recv,
):
    d, z, x, c = place()
    other = 1 - c
    active = z < 6
    near = d // 4 == c
    half = pl.ds(4 * c, 4)

    @pl.when(active)
    def _():
        give = remote(part.at[pl.ds(4 * other, 4)], in_sib, s_send.at[0], s_recv.at[0], d, z, x, other)
        give.start()
        keep = pltpu.make_async_copy(part.at[half], half_sum, l_sem.at[0])
        keep.start()
        keep.wait()
        give.wait()

        @pl.loop(0, 4)
        def _(k):
            half_sum[k] = half_sum[k] + in_sib[k]

        def x_copy(step):
            to = (x + step) % 4
            return remote(half_sum.at[:, :, to], in_x.at[step], x_send.at[step], x_recv.at[step], d, z, to, c)

        for step in range(1, 4):
            x_copy(step).start()
        for step in range(1, 4):
            x_copy(step).wait_recv()
        @pl.loop(0, 4)
        def _(k):
            x_sum[k] = (half_sum[k, :, x] + in_x[1, k]) + (in_x[2, k] + in_x[3, k])

        def y_copy(k):
            return remote(x_sum.at[k], in_y.at[d], y_send.at[k], y_recv.at[d], 4 * c + k, z, x, c)

        for k in range(4):
            @pl.when(4 * c + k != d)
            def _():
                y_copy(k).start()

        @pl.when(near)
        def _():
            for s in range(8):
                @pl.when(d != s)
                def _():
                    pltpu.make_async_copy(in_y.at[s], in_y.at[s], y_recv.at[s]).wait()
            total = x_sum[d % 4]
            for step in range(1, 8):
                total = total + in_y[(d + step) % 8]
            y_sum[...] = total

            for step in range(1, 8):
                to = (z + step) % 8
                remote(y_sum.at[to], in_z.at[z], z_send.at[step], z_recv.at[z], d, to, x, c).start()

        for k in range(4):
            @pl.when(4 * c + k != d)
            def _():
                y_copy(k).wait_send()
        for step in range(1, 4):
            x_copy(step).wait_send()

    echo = remote(done, got, e_send.at[0], e_recv.at[0], d, z, x, other)

    @pl.when(near)
    def _():
        @pl.when(active)
        def _():
            in_z[z] = y_sum[z]

        for s in range(6):
            @pl.when(z != s)
            def _():
                pltpu.make_async_copy(in_z.at[s], in_z.at[s], z_recv.at[s]).wait()
        total = in_z[0]
        for s in range(1, 6):
            total = total + in_z[s]
        done[...] = total / 768.0
        echo.start()
        out[...] = done[...]

        @pl.when(active)
        def _():
            for step in range(1, 8):
                to = (z + step) % 8
                remote(y_sum.at[to], in_z.at[z], z_send.at[step], z_recv.at[z], d, to, x, c).wait_send()
        echo.wait_send()

    @pl.when(jnp.logical_not(near))
    def _():
        echo.wait_recv()
        out[...] = got[...]


def collect(part):
    dma = pltpu.SemaphoreType.DMA
    vmem = lambda *shape: pltpu.VMEM(shape, F32)
    return pl.pallas_call(
        collect_kernel,
        out_shape=jax.ShapeDtypeStruct((8, 128), F32),
        in_specs=[ANY],
        out_specs=pl.BlockSpec(memory_space=pltpu.VMEM),
        scratch_shapes=[
            vmem(8, 128),
            vmem(4, 8, 4, 8, 128), vmem(4, 8, 4, 8, 128),
            vmem(4, 4, 8, 8, 128), vmem(4, 8, 8, 128),
            vmem(8, 8, 8, 128), vmem(8, 8, 128),
            vmem(8, 8, 128), vmem(8, 128),
            dma((1,)), dma((1,)), dma((1,)), dma((4,)), dma((4,)), dma((4,)), dma((8,)),
            dma((8,)), dma((8,)), dma((1,)), dma((1,)),
        ],
        compiler_params=pltpu.CompilerParams(
            has_side_effects=True, vmem_limit_bytes=24 * 2**20
        ),
        name="collect",
    )(part)


def per_device(surface, refl, pool, tile_ids, block_ids, counts):
    d = lax.axis_index("depth")
    own = lax.dynamic_slice_in_dim(surface, d * 16, 16, 2)
    own = own.reshape(3, 2, 8, 2, 8, 128)
    wsrc = jnp.transpose(own, (0, 2, 3, 1, 4, 5)).reshape(3, 8, 32, 128)
    scale = 1.0 / jnp.sqrt(counts[0].astype(F32))
    fac = (1.0 - refl.reshape(8, 128)) * scale[:, None]
    live = jnp.arange(10)[None, :] < counts[0][:, None]
    slots = jnp.where(live, block_ids[0] * 1024 + tile_ids[0] * 4, DEAD)
    ints = jnp.concatenate(
        [slots.T.reshape(1, 80), jnp.max(counts).reshape(1, 1), jnp.zeros((1, 47), jnp.int32)], 1
    ).astype(jnp.int32)
    wave, fac_all, ints_all, pool_all = spread(wsrc, fac, ints, pool)
    part = levels(
        ints_all.reshape(8, 32, 128), wave, fac_all.reshape(8, 256, 128), pool_all
    )
    return collect(part.reshape(8, 8, 4, 8, 128)).reshape(1, 1024)


def solution(mesh):
    placed = (
        P("freq", None, None, "lat"),
        P("depth", "lat"),
        P("depth", "freq", None, None, None),
        P("depth", "lat", None),
        P("depth", "lat", None),
        P("depth", "lat"),
    )
    return jax.shard_map(
        per_device, mesh=mesh, in_specs=placed, out_specs=P("depth", "lat"), check_vma=False
    )
```

time: 463 us -> 176 us (0.38)
  the two profiles are of different devices: /device:TPU:57 before, /device:TPU:1 now
where the time goes in v1:
time: 176 us
  Pallas kernels  163 us (93%)
  local copies, waits for them, and re-layouts  6.8 us (4%)
  other arithmetic  5.51 us (3%)
    pallas_call x1, Pallas kernels, spread(): pl.pallas_call(spread_kernel, out_shape=(jax.ShapeDtypeStruct((32, 32, 12...  67.1 us
    pallas_call x1, Pallas kernels, levels(): pl.pallas_call(levels_kernel, grid=(8,), out_shape=jax.ShapeDtypeStruct((...  52.5 us
    pallas_call x1, Pallas kernels, collect(): pl.pallas_call(collect_kernel, out_shape=jax.ShapeDtypeStruct((8, 128), F...  43.5 us
    unnamed x12, local copies, waits for them, and re-layouts  5.89 us

profile of v1, /device:TPU:1, one launch (start us, length us, event | category | flops | bytes accessed | tf_op | source)
XLA Modules:
  0.0 175.5 jit_solution(14154514476807966995)
XLA Ops:
  0.0 0.0 copy-start
  0.0 1.4 reduce_max.9
  1.4 0.7 convert_rsqrt_fusion
  2.1 0.7 broadcast_subtract_fusion
  2.8 0.7 broadcast_multiply_fusion.fac
  3.5 0.8 fusion
  4.2 0.1 copy.9
  4.3 0.1 reshape.41
  4.4 1.3 bitcast_add_fusion.ints
  5.7 0.0 copy-done
  5.7 0.7 copy.8
  6.5 67.1 %spread.1 = (bf16[32,32,128]{2,1,0:T(8,128)(2,1)}, f32[8,8,4,8,128]{4,3,2,1,0:T(8,128)}, s32[8,8,4,1,128]{4,3,2,1,0:T(1,128)}, bf16[8,8,128,256]{3,2,1,0:T(8,128)(2,1)}) custom-call(bf16[3,8,32,128]{3,2,1,0:T(8,128)(2,1)} %bitcast.30, f32[8,128]{1,0:T(8,128)} %broadcast_multiply_fusion.fac, s32[1,128]{1,0:T(1,128)} %bitcast_add_fusion.ints, ...), custom_call_target="tpu_custom_call" | custom-call | tf_op jit(solution)/shard_map/spread/pallas_call | solution.py:243
  73.6 0.0 copy-start.1
  73.6 2.2 %copy-done.1 = bf16[8,8,128,256]{3,2,1,0:T(8,128)(2,1)S(1)} copy-done((bf16[8,8,128,256]{3,2,1,0:T(8,128)(2,1)S(1)}, bf16[8,8,128,256]{3,2,1,0:T(8,128)(2,1)}, u32[]{:S(2)}) %copy-start.1) | copy-done | bytes 4194328
  75.8 0.0 copy-start.2
  75.8 1.2 copy-done.2
  77.0 0.0 copy-start.3
  77.0 0.9 copy-done.3
  78.0 0.0 copy-start.4
  78.0 0.9 copy-done.4
  78.9 52.5 %levels.1 = f32[8,256,128]{2,1,0:T(8,128)S(1)} custom-call(s32[8,32,128]{2,1,0:T(8,128)S(1)} %bitcast.26, bf16[32,32,128]{2,1,0:T(8,128)(2,1)S(1)} %copy-done.3, f32[8,256,128]{2,1,0:T(8,128)S(1)} %bitcast.25, bf16[8,8,128,256]{3,2,1,0:T(8,128)(2,1)S(1)} %copy-done.1), custom_call_target="tpu_custom_call" | custom-call | tf_op jit(solution)/shard_map/levels/pallas_call | solution.py:332
  131.4 43.5 %collect.1 = f32[8,128]{1,0:T(8,128)S(1)} custom-call(f32[8,8,4,8,128]{4,3,2,1,0:T(8,128)S(1)} %bitcast.24), custom_call_target="tpu_custom_call" | custom-call | tf_op jit(solution)/shard_map/collect/pallas_call | solution.py:453
  174.9 0.6 copy.12
  (3 shorter events, 0.0 us)
Async XLA Ops:
  0.0 5.7 %copy-start = (bf16[3,2,128,1024]{3,2,1,0:T(8,128)(2,1)S(1)}, bf16[3,2,128,1024]{3,2,1,0:T(8,128)(2,1)}, u32[]{:S(2)}) copy-start(bf16[3,2,128,1024]{3,2,1,0:T(8,128)(2,1)} %param.6) | copy-start | bytes 4718596
  73.6 2.2 %copy-start.1 = (bf16[8,8,128,256]{3,2,1,0:T(8,128)(2,1)S(1)}, bf16[8,8,128,256]{3,2,1,0:T(8,128)(2,1)}, u32[]{:S(2)}) copy-start(bf16[8,8,128,256]{3,2,1,0:T(8,128)(2,1)} %get-tuple-element.12.pool) | copy-start | bytes 12582916
  75.8 1.2 copy-start.2
  77.0 0.9 copy-start.3
  78.0 0.9 copy-start.4

commit v2 on v1

--- a/solution.py
+++ b/solution.py
@@ -28,6 +28,13 @@
         device_id=(d, z * 4 + x, c),
         device_id_type=MESH,
     )
+
+
+def greet(peers):
+    barrier = pltpu.get_barrier_semaphore()
+    for d, z, x, c in peers:
+        pl.semaphore_signal(barrier, inc=1, device_id=(d, z * 4 + x, c), device_id_type=MESH)
+    pl.semaphore_wait(barrier, len(peers))
 
 
 def spread_kernel(
@@ -41,6 +48,12 @@
     active = z < 6
     own_core = z // 3
     half = pl.ds(4 * c, 4)
+
+    greet(
+        [(d, (z + i) % 8, (x + j) % 4, c) for i in range(8) for j in range(4) if i or j]
+        + [(d, (z + i) % 8, (x + j) % 4, other) for i in range(8) for j in range(4)]
+        + [((d + i) % 8, z, x, c) for i in range(1, 8)]
+    )
 
     mine = pool.at[0, z % 3]
     here = pltpu.make_async_copy(mine, pool_all.at[d], l_sem.at[0])
@@ -256,7 +269,7 @@
             dma((2,)), dma((2,)),
             dma((2, 4)), dma((2, 4)), dma((8,)), dma((8,)), dma((4,)),
         ],
-        compiler_params=pltpu.CompilerParams(has_side_effects=True),
+        compiler_params=pltpu.CompilerParams(has_side_effects=True, collective_id=1),
         name="spread",
     )(wsrc, fac, ints, pool)
 
@@ -295,18 +308,25 @@
                     base = (2 * pair + k) * 1024 + q
                     prod[pl.ds(base, 256, stride=4), :] = out[:, 128 * k : 128 * k + 128]
 
-        @pl.loop(0, 32)
+        @pl.loop(0, 16)
         def _(g):
-            most = ints[level, g, 80]
-
-            def slot(k, sums):
-                return tuple(
-                    sums[r] + prod[pl.ds(ints[level, g, k * 8 + r], 4), :] for r in range(8)
-                )
-
-            sums = lax.fori_loop(0, most, slot, tuple(jnp.zeros((4, 128), F32) for _ in range(8)))
-            for r in range(8):
-                rows[pl.ds(pl.multiple_of(g * 32, 32) + 4 * r, 4), :] = sums[r]
+            most = jnp.maximum(ints[level, 2 * g, 80], ints[level, 2 * g + 1, 80])
+
+            def add(slots):
+                for r in range(16):
+                    at = [ints[level, 2 * g + r // 8, k * 8 + r % 8] for k in range(slots)]
+                    parts = [prod[pl.ds(i, 4), :] for i in at]
+                    while len(parts) > 1:
+                        parts = [sum(parts[i : i + 2]) for i in range(0, len(parts), 2)]
+                    rows[pl.ds(pl.multiple_of(g * 64, 64) + 4 * r, 4), :] = parts[0]
+
+            @pl.when(most <= 5)
+            def _():
+                add(5)
+
+            @pl.when(most > 5)
+            def _():
+                add(10)
 
         @pl.loop(0, 16)
         def _(i):
@@ -345,7 +365,7 @@
             pltpu.VMEM((DEAD + 8, 128), F32),
             pltpu.VMEM((1024, 128), F32),
         ],
-        compiler_params=pltpu.CompilerParams(vmem_limit_bytes=40 * 2**20),
+        compiler_params=pltpu.CompilerParams(vmem_limit_bytes=60 * 2**20),
         name="levels",
     )(ints, wave, fac, pool)
 
@@ -359,6 +379,13 @@
     active = z < 6
     near = d // 4 == c
     half = pl.ds(4 * c, 4)
+
+    greet(
+        [(d, z, x, other)]
+        + [(d, z, (x + i) % 4, c) for i in range(1, 4)]
+        + [(d, (z + i) % 8, x, c) for i in range(1, 8)]
+        + [((d + i) % 8, z, x, c) for i in range(1, 8)]
+    )
 
     @pl.when(active)
     def _():
@@ -465,7 +492,7 @@
             dma((8,)), dma((8,)), dma((1,)), dma((1,)),
         ],
         compiler_params=pltpu.CompilerParams(
-            has_side_effects=True, vmem_limit_bytes=24 * 2**20
+            has_side_effects=True, vmem_limit_bytes=60 * 2**20, collective_id=2
         ),
         name="collect",
     )(part)

time: 176 us -> 125 us (0.71)
  Pallas kernels: 163 us -> 117 us
  local copies, waits for them, and re-layouts: 6.8 us -> 2.2 us
    pallas_call x1, Pallas kernels: 52.5 us -> 26.1 us  [levels(): pl.pallas_call(levels_kernel, grid=(8,), out_shape=jax.ShapeDtypeStruct((...]
    pallas_call x1, Pallas kernels: 43.5 us -> 28.9 us  [collect(): pl.pallas_call(collect_kernel, out_shape=jax.ShapeDtypeStruct((8, 128), F...]
    pallas_call x1, Pallas kernels: 67.1 us -> 61.6 us  [spread(): pl.pallas_call(spread_kernel, out_shape=(jax.ShapeDtypeStruct((32, 32, 12...]
    unnamed x12 -> x4, local copies, waits for them, and re-layouts: 5.89 us -> 1.31 us
where the time goes in v2:
time: 125 us; the launch traced here: 124 us
  Pallas kernels  117 us (94%)
  other arithmetic  5.63 us (5%)
  local copies, waits for them, and re-layouts  2.2 us (2%)
    pallas_call x1, Pallas kernels, spread(): pl.pallas_call(spread_kernel, out_shape=(jax.ShapeDtypeStruct((32, 32, 12...  61.6 us
    pallas_call x1, Pallas kernels, collect(): pl.pallas_call(collect_kernel, out_shape=jax.ShapeDtypeStruct((8, 128), F...  28.9 us
    pallas_call x1, Pallas kernels, levels(): pl.pallas_call(levels_kernel, grid=(8,), out_shape=jax.ShapeDtypeStruct((...  26.1 us

profile of v2, /device:TPU:1, one launch (start us, length us, event | category | flops | bytes accessed | tf_op | source)
XLA Modules:
  0.0 124.5 jit_solution(833130662782727232)
XLA Ops:
  0.0 0.0 copy-start
  0.0 1.5 %reduce_max.9 = s32[]{:T(128)} reduce(s32[1,8]{1,0:T(1,128)} %param.11, s32[]{:T(128)} %constant.9.clone.1), dimensions={0,1}, to_apply=%region_0.1 | reduce | flops 7 | bytes 40 | tf_op jit(solution)/shard_map/reduce_max | solution.py:511
  1.5 0.7 convert_rsqrt_fusion
  2.2 0.7 broadcast_subtract_fusion
  2.9 0.7 broadcast_multiply_fusion.fac
  3.5 0.8 fusion
  4.3 0.1 copy.9
  4.4 0.1 reshape.41
  4.5 1.3 %bitcast_add_fusion.ints = s32[1,128]{1,0:T(1,128)} fusion(s32[47]{0:T(128)S(1)} %broadcast_in_dim.10, s32[1,1]{1,0:T(1,128)} %bitcast.6, s32[1,80]{1,0:T(1,128)S(1)} %reshape.41), kind=kLoop, calls=%fused_computation.5 | loop fusion | flops 256 | bytes 1024 | tf_op jit(solution)/shard_map/concatenate | solution.py:510
  5.8 0.0 copy-done
  5.9 0.7 copy.8
  6.6 61.6 %spread.1 = (bf16[32,32,128]{2,1,0:T(8,128)(2,1)}, f32[8,8,4,8,128]{4,3,2,1,0:T(8,128)}, s32[8,8,4,1,128]{4,3,2,1,0:T(1,128)}, bf16[8,8,128,256]{3,2,1,0:T(8,128)(2,1)}) custom-call(bf16[3,8,32,128]{3,2,1,0:T(8,128)(2,1)} %bitcast.28, f32[8,128]{1,0:T(8,128)} %broadcast_multiply_fusion.fac, s32[1,128]{1,0:T(1,128)} %bitcast_add_fusion.ints, ...), custom_call_target="tpu_custom_call" | custom-call | tf_op jit(solution)/shard_map/spread/pallas_call | solution.py:256
  68.2 26.1 %levels.1 = f32[8,256,128]{2,1,0:T(8,128)} custom-call(s32[8,32,128]{2,1,0:T(8,128)} %bitcast.29, bf16[32,32,128]{2,1,0:T(8,128)(2,1)} %get-tuple-element.10.wave, f32[8,256,128]{2,1,0:T(8,128)} %bitcast.25, bf16[8,8,128,256]{3,2,1,0:T(8,128)(2,1)} %get-tuple-element.12.pool), custom_call_target="tpu_custom_call" | custom-call | tf_op jit(solution)/shard_map/levels/pallas_call | solution.py:352
  94.3 28.9 %collect.1 = f32[8,128]{1,0:T(8,128)} custom-call(f32[8,8,4,8,128]{4,3,2,1,0:T(8,128)} %bitcast.24), custom_call_target="tpu_custom_call" | custom-call | tf_op jit(solution)/shard_map/collect/pallas_call | solution.py:480
  123.2 1.3 %copy.12 = f32[1,1024]{1,0:T(1,128)} copy(f32[1,1024]{1,0:T(1,128)} %bitcast.30) | data formatting | bytes 8192
  (3 shorter events, 0.0 us)
Async XLA Ops:
  0.0 5.8 %copy-start = (bf16[3,2,128,1024]{3,2,1,0:T(8,128)(2,1)S(1)}, bf16[3,2,128,1024]{3,2,1,0:T(8,128)(2,1)}, u32[]{:S(2)}) copy-start(bf16[3,2,128,1024]{3,2,1,0:T(8,128)(2,1)} %param.6) | copy-start | bytes 4718596

commit v3 on v0

v3 whole, which is shorter than its diff:
```python
import jax
import jax.numpy as jnp
from jax import lax
from jax.experimental import pallas as pl
from jax.experimental.pallas import tpu as pltpu
from jax.sharding import PartitionSpec as P

MESH = pl.DeviceIdType.MESH
ANY = pl.BlockSpec(memory_space=pl.ANY)
VMEM = pl.BlockSpec(memory_space=pltpu.VMEM)
BF = jnp.bfloat16
F32 = jnp.float32
WIDE = 144
DEAD = 8 * WIDE


def remote(src, dst, send, recv, d, z, x, c):
    return pltpu.make_async_remote_copy(
        src_ref=src,
        dst_ref=dst,
        send_sem=send,
        recv_sem=recv,
        device_id=(d, z * 4 + x, c),
        device_id_type=MESH,
    )


def arrival(ref, sem):
    return pltpu.make_async_copy(ref, ref, sem)


def turned(rows):
    count = rows.shape[0]
    even = lax.broadcasted_iota(jnp.int32, rows.shape, 0) % 2 == 0
    return jnp.where(even, -pltpu.roll(rows, count - 1, 0), pltpu.roll(rows, 1, 0))


def kernel(
    wsrc, fac, ints, pool, out,
    wave, field, pool_all, fac_all, ints_all, lists, prod, img, in_x, x_sum, in_yz, done, got,
    l_sem, w_send, w_recv, y_send, y_recv, z_send, z_recv, x_send, x_recv,
    p_send, p_recv, q_send, q_recv, h_send, h_recv, i_send, i_recv, o_send, o_recv, e_sem,
):
    d = lax.axis_index("depth")
    a = lax.axis_index("lat")
    c = lax.axis_index("freq")
    z, x = a // 4, a % 4
    other = 1 - c
    active = z < 6
    side = z // 4
    near = side == c
    source = z // 3
    gives = jnp.logical_and(active, c == source)
    takes = jnp.logical_and(active, c != source)
    half = pl.ds(4 * c, 4)

    def wave_out(i):
        return 3 * c + i // 4, i % 4, side

    def wave_in(i):
        return 4 * c + i // 4, i % 4, source

    def is_me(tz, tx, tc):
        return jnp.logical_and(tz * 4 + tx == a, tc == c)

    def wave_copy(i):
        tz, tx, tc = wave_out(i)
        return remote(
            wsrc.at[i // 4, i % 4], wave.at[a % 16], w_send.at[i], w_recv.at[a % 16], d, tz, tx, tc
        )

    slot = x * 4 + z % 4

    def y_copies(step):
        to = (d + step) % 8
        return (
            remote(fac, fac_all.at[d, slot], y_send.at[0, step], y_recv.at[0, step], to, z, x, c),
            remote(ints, ints_all.at[d, slot], y_send.at[1, step], y_recv.at[1, step], to, z, x, c),
        )

    def z_copies(step):
        to = (z + step) % 8
        return to, [
            remote(whole.at[:, slot], whole.at[:, slot], z_send.at[kind, step], z_recv.at[kind, z % 4], d, to, x, c)
            for kind, whole in ((0, fac_all), (1, ints_all))
        ]

    def x_copies(step):
        to = (x + step) % 4
        column = pl.ds(4 * x, 4)
        return [
            remote(whole.at[:, column], whole.at[:, column], x_send.at[kind, step], x_recv.at[kind, step], d, z, to, c)
            for kind, whole in ((0, fac_all), (1, ints_all))
        ]

    def ring_copy(way, step):
        if way == 0:
            level, to = (d - step + 8) % 8, (d + 1) % 8
        else:
            level, to = (d + step) % 8, (d + 7) % 8
        at = pool_all.at[level, half]
        return remote(at, at, p_send.at[way, step], p_recv.at[way, step], to, z, x, c)

    def share(way, step):
        level = (d - 1 - step + 8) % 8 if way == 0 else (d + 1 + step) % 8
        at = pool_all.at[level, half]
        return remote(at, at, q_send.at[way, step], q_recv.at[way, step], d, z, x, other)

    mine = pool.at[0, z % 3]
    here = pltpu.make_async_copy(mine, pool_all.at[d], l_sem.at[0])
    over = remote(mine, pool_all.at[d], q_send.at[1, 3], q_recv.at[1, 3], d, z, x, other)

    def edges(way, parity):
        own, theirs = ((64, 1088), (1024, 0))[way]
        return remote(
            field.at[parity, pl.ds(own, 64)], field.at[parity, pl.ds(theirs, 64)],
            h_send.at[parity, way], h_recv.at[parity, way], d, z, x, other,
        )

    barrier = pltpu.get_barrier_semaphore()

    def greet(d, z, x, c):
        pl.semaphore_signal(barrier, inc=1, device_id=(d, z * 4 + x, c), device_id_type=MESH)

    greet(d, z, x, other)
    for i in range(1, 8):
        greet((d + i) % 8, z, x, c)
        greet(d, (z + i) % 8, x, c)
    for i in range(1, 4):
        greet(d, z, (x + i) % 4, c)

    @pl.loop(0, 12)
    def _(i):
        @pl.when(jnp.logical_not(is_me(*wave_out(i))))
        def _():
            greet(d, *wave_out(i))

    @pl.when(active)
    def _():
        @pl.loop(0, 16)
        def _(i):
            @pl.when(jnp.logical_not(is_me(*wave_in(i))))
            def _():
                greet(d, *wave_in(i))

    loops = jnp.logical_and(gives, near).astype(jnp.int32)
    pl.semaphore_wait(barrier, 18 + 12 - loops + jnp.where(active, 16 - loops, 0))

    @pl.when(gives)
    def _():
        over.start()
        here.start()

    @pl.when(near)
    def _():
        fac_all[d, slot] = fac[...]
        ints_all[d, slot] = ints[...]
        for step in range(1, 8):
            for copy in y_copies(step):
                copy.start()

    @pl.loop(0, 12)
    def _(i):
        same = is_me(*wave_out(i))

        @pl.when(same)
        def _():
            pltpu.make_async_copy(wsrc.at[i // 4, i % 4], wave.at[a % 16], l_sem.at[1]).start()

        @pl.when(jnp.logical_not(same))
        def _():
            wave_copy(i).start()

    @pl.when(gives)
    def _():
        here.wait()

    @pl.when(takes)
    def _():
        over.wait_recv()

    @pl.when(active)
    def _():
        ring_copy(0, 0).start()
        ring_copy(1, 0).start()

    @pl.when(near)
    def _():
        for step in range(1, 8):
            for copy in y_copies(step):
                copy.wait_recv()
        for step in range(1, 8):
            to, copies = z_copies(step)

            @pl.when(to < 6)
            def _():
                for copy in copies:
                    copy.start()

    def ring_step(step):
        for way in range(2):
            if step < 4 - way:
                ring_copy(way, step).wait_recv()
                if step < 3 - way:
                    ring_copy(way, step + 1).start()
                share(way, step).start()

    @pl.when(active)
    def _():
        ring_step(0)

        @pl.loop(0, 16)
        def _(i):
            same = is_me(*wave_in(i))

            @pl.when(same)
            def _():
                arrival(wave.at[i], l_sem.at[1]).wait()

            @pl.when(jnp.logical_not(same))
            def _():
                arrival(wave.at[i], w_recv.at[i]).wait()

            at = pl.ds(pl.multiple_of(64 + 64 * i, 64), 64)
            rows = wave[i]
            field[0, at, :128] = rows
            field[0, at, 128:] = turned(rows.astype(F32)).astype(BF)

        edges(0, 0).start()
        edges(1, 0).start()
        prod[DEAD] = jnp.zeros((8, 128), F32)

        for k in range(4):
            @pl.when(4 * c + k != z)
            def _():
                for kind, whole in ((0, fac_all), (1, ints_all)):
                    arrival(whole.at[:, 4 * x + k], z_recv.at[kind, k]).wait()
        for step in range(1, 4):
            for copy in x_copies(step):
                copy.start()

        ring_step(1)
        for step in range(1, 4):
            for copy in x_copies(step):
                copy.wait_recv()
        to_scalars = pltpu.make_async_copy(ints_all, lists, l_sem.at[2])
        to_scalars.start()
        ring_step(2)
        ring_step(3)
        to_scalars.wait()
        for way in range(2):
            for step in range(4 - way):
                share(way, step).wait_recv()

        def image_copy(level, step):
            to = (x + step) % 4
            return remote(
                img.at[level, pl.ds(4 * to, 4)], in_x.at[step, level],
                i_send.at[level, step], i_recv.at[level, step], d, z, to, c,
            )

        def owner_copy(level, k):
            return remote(
                x_sum.at[level, k], in_yz.at[d, z], o_send.at[level, k], o_recv.at[d, z],
                level, 4 * c + k, x, c,
            )

        def is_owner(level, k):
            return jnp.logical_and(level == d, 4 * c + k == z)

        def hand_in(level):
            for step in range(1, 4):
                image_copy(level, step).wait_recv()
            x_sum[level] = (img[level, pl.ds(4 * x, 4)] + in_x[1, level]) + (
                in_x[2, level] + in_x[3, level]
            )
            for k in range(4):
                @pl.when(is_owner(level, k))
                def _():
                    in_yz[d, z] = x_sum[level, k]

                @pl.when(jnp.logical_not(is_owner(level, k)))
                def _():
                    owner_copy(level, k).start()

        def group(level, now, g):
            later = 1 - now
            for m in range(8):
                new = []
                for r in (2 * m, 2 * m + 1):
                    block = 2 * g + r // 8
                    at = (block % 4) * 4 + block // 4
                    parts = [prod[lists[level, at, 0, k * 8 + r % 8]] for k in range(10)]
                    while len(parts) > 1:
                        parts = [sum(parts[i + 1 : i + 2], parts[i]) for i in range(0, len(parts), 2)]
                    row = parts[0] * fac_all[level, at, r % 8 : r % 8 + 1, :]
                    img[level, at, r % 8 : r % 8 + 1, :] = jnp.sum(row * row, axis=0, keepdims=True)
                    new.append(row)
                pair = jnp.concatenate(new, 0)
                at = pl.ds(pl.multiple_of(64 + 128 * g + 16 * m, 16), 16)
                field[later, at, :128] = pair.astype(BF)
                field[later, at, 128:] = turned(pair).astype(BF)

        @pl.loop(0, 8)
        def _(level):
            now = level % 2
            for way in range(2):
                edges(way, now).wait()
            for p in range(4):
                b0, b1 = pool_all[level, 2 * p], pool_all[level, 2 * p + 1]
                weights = jnp.concatenate(
                    [
                        jnp.concatenate([b0[:, :128], b1[:, :128]], 1),
                        jnp.concatenate([b0[:, 128:], b1[:, 128:]], 1),
                    ],
                    0,
                )
                product = jnp.dot(field[now], weights, preferred_element_type=F32)
                for k in range(2):
                    prod[pl.ds((2 * p + k) * WIDE, WIDE)] = product[
                        :, 128 * k : 128 * k + 128
                    ].reshape(WIDE, 8, 128)

            @pl.loop(0, 2)
            def _(i):
                group(level, now, 7 * i)

            @pl.when(level < 7)
            def _():
                for way in range(2):
                    edges(way, 1 - now).start()

            @pl.loop(1, 7)
            def _(g):
                group(level, now, g)

            for step in range(1, 4):
                image_copy(level, step).start()

            @pl.when(level > 0)
            def _():
                hand_in(level - 1)

        hand_in(7)

        @pl.loop(0, 8)
        def _(level):
            for step in range(1, 4):
                image_copy(level, step).wait_send()
            for k in range(4):
                @pl.when(jnp.logical_not(is_owner(level, k)))
                def _():
                    owner_copy(level, k).wait_send()

    echo = remote(done, got, e_sem.at[0], e_sem.at[1], d, z, x, other)

    @pl.when(near)
    def _():
        def add(i, total):
            fd, fz = i // 6, i % 6

            @pl.when(jnp.logical_or(fd != d, fz != z))
            def _():
                arrival(in_yz.at[fd, fz], o_recv.at[fd, fz]).wait()

            return total + in_yz[fd, fz]

        done[...] = lax.fori_loop(0, 48, add, jnp.zeros((8, 128), F32)) / 768.0
        echo.start()
        out[...] = done[...]
        echo.wait_send()

    @pl.when(jnp.logical_not(near))
    def _():
        echo.wait_recv()
        out[...] = got[...]

    @pl.when(near)
    def _():
        for step in range(1, 8):
            for copy in y_copies(step):
                copy.wait_send()
            to, copies = z_copies(step)

            @pl.when(to < 6)
            def _():
                for copy in copies:
                    copy.wait_send()

    @pl.loop(0, 12)
    def _(i):
        @pl.when(jnp.logical_not(is_me(*wave_out(i))))
        def _():
            wave_copy(i).wait_send()

    @pl.when(gives)
    def _():
        over.wait_send()

    @pl.when(active)
    def _():
        for step in range(1, 4):
            for copy in x_copies(step):
                copy.wait_send()
        for way in range(2):
            for step in range(4 - way):
                ring_copy(way, step).wait_send()
                share(way, step).wait_send()


def run(wsrc, fac, ints, pool):
    dma = pltpu.SemaphoreType.DMA
    vmem = pltpu.VMEM
    return pl.pallas_call(
        kernel,
        out_shape=jax.ShapeDtypeStruct((8, 128), F32),
        in_specs=[VMEM, VMEM, VMEM, ANY],
        out_specs=VMEM,
        scratch_shapes=[
            vmem((16, 64, 128), BF),
            vmem((2, 8 * WIDE, 256), BF),
            vmem((8, 8, 128, 256), BF),
            vmem((8, 16, 8, 128), F32),
            vmem((8, 16, 1, 128), jnp.int32),
            pltpu.SMEM((8, 16, 1, 128), jnp.int32),
            vmem((DEAD + 1, 8, 128), F32),
            vmem((8, 16, 8, 128), F32),
            vmem((4, 8, 4, 8, 128), F32),
            vmem((8, 4, 8, 128), F32),
            vmem((8, 8, 8, 128), F32),
            vmem((8, 128), F32),
            vmem((8, 128), F32),
            dma((3,)), dma((12,)), dma((16,)),
            dma((2, 8)), dma((2, 8)), dma((2, 8)), dma((2, 4)), dma((2, 4)), dma((2, 4)),
            dma((2, 4)), dma((2, 4)), dma((2, 4)), dma((2, 4)),
            dma((2, 2)), dma((2, 2)), dma((8, 4)), dma((8, 4)), dma((8, 4)), dma((8, 8)), dma((2,)),
        ],
        compiler_params=pltpu.CompilerParams(
            has_side_effects=True, collective_id=1, vmem_limit_bytes=48 * 2**20
        ),
        name="levels",
    )(wsrc, fac, ints, pool)


def per_device(surface, refl, pool, tile_ids, block_ids, counts):
    d = lax.axis_index("depth")
    first = 128 * (lax.axis_index("lat") // 16)
    own = lax.dynamic_slice_in_dim(surface, d * 16, 16, 2)
    own = own.reshape(3, 2, 4, 4, 8, 128)
    wsrc = jnp.transpose(own, (0, 2, 4, 3, 1, 5)).reshape(3, 4, 64, 128)
    scale = 1.0 / jnp.sqrt(counts[0].astype(F32))
    fac = (1.0 - refl.reshape(8, 128)) * scale[:, None]
    live = jnp.arange(10)[None, :] < counts[0][:, None]
    slots = jnp.where(live, block_ids[0] * WIDE + (tile_ids[0] - first + 8) % 256, DEAD)
    ints = jnp.concatenate([slots.T.reshape(1, 80), jnp.zeros((1, 48), jnp.int32)], 1)
    return run(wsrc, fac, ints.astype(jnp.int32), pool).reshape(1, 1024)


def solution(mesh):
    placed = (
        P("freq", None, None, "lat"),
        P("depth", "lat"),
        P("depth", "freq", None, None, None),
        P("depth", "lat", None),
        P("depth", "lat", None),
        P("depth", "lat"),
    )
    return jax.shard_map(
        per_device, mesh=mesh, in_specs=placed, out_specs=P("depth", "lat"), check_vma=False
    )
```

time: 463 us -> 88.5 us (0.19); the launches traced: 457 us -> 88.3 us
  local copies, waits for them, and re-layouts: 114 us -> 2.81 us
  waiting for transfers between devices: 111 us -> 0 us
  Pallas kernels: 0 us -> 83.1 us
  starting transfers between devices: 76.4 us -> 0 us
  matrix products: 64.4 us -> 0 us
  blocking collectives: 38.1 us -> 0 us
  other arithmetic: 38.8 us -> 2.32 us
  between operations: 13.4 us -> 0.04 us
    all_gather x1 -> x0, waiting for transfers between devices: 110 us -> none  [per_device(): pool_all = lax.all_gather(pool, 'depth', axis=0, tiled=True)]
    gather x16 -> x0, local copies, waits for them, and re-layouts: 84.6 us -> none  [the longest x8 65.3 us: extrapolate(): chosen = jnp.take(pool_level, block_level, axis=1)]
    pallas_call x0 -> x1, Pallas kernels: none -> 83.1 us  [run(): pl.pallas_call(kernel, out_shape=jax.ShapeDtypeStruct((8, 128), F32), in_...]
    ppermute x16 -> x0, starting transfers between devices: 70.1 us -> none  [the longest x8 54.7 us: extended_2(): lax.ppermute(lax.slice_in_dim(block, 0, width, axis=dim), axis, backward)]
    dot_general x8 -> x0, matrix products: 64.4 us -> none  [extrapolate(): jnp.einsum('fsarkt,frktc->rfsac', picked, chosen, preferred_element_type=...]
    all_gather x1 -> x0, blocking collectives: 19.8 us -> none  [in_one_piece(): lax.all_gather(both, axis, axis=dim, tiled=True)]
    squeeze x8 -> x0, local copies, waits for them, and re-layouts: 12.1 us -> none  [level_step(): lax.dynamic_index_in_dim(pool_all, level_index, 0, keepdims=False)]
    dynamic_update_slice x8 -> x0, local copies, waits for them, and re-layouts: 11.1 us -> none  [level_step(): lax.dynamic_update_index_in_dim(images, partial_value, level_index, 0)]
  transfers between devices with their start and end apart: 18 -> 0, of which waited for: 1 -> 0; matrix products, arithmetic and copies ran while one was open for 24% -> 0% of each run, Pallas kernels for 0% -> 0%
where the time goes in v3:
time: 88.5 us; the launch traced here: 88.3 us
  Pallas kernels  83.1 us (94%)
  local copies, waits for them, and re-layouts  2.81 us (3%)
  other arithmetic  2.32 us (3%)
    pallas_call x1, Pallas kernels, run(): pl.pallas_call(kernel, out_shape=jax.ShapeDtypeStruct((8, 128), F32), in_...  83.1 us
    unnamed x6, local copies, waits for them, and re-layouts  2.42 us

profile of v3, /device:TPU:57, one launch (start us, length us, event | category | flops | bytes accessed | tf_op | source)
XLA Modules:
  0.0 88.3 jit_solution(13211101601185296032)
XLA Ops:
  0.0 0.0 copy-start
  0.0 0.9 %fusion.3 = s32[10,8]{0,1:T(8,128)S(1)} fusion(s32[1,8,10]{2,1,0:T(8,128)} %param.10, s32[1,8,10]{2,1,0:T(8,128)} %param.9, s32[]{:T(128)S(6)} %mul.29, s32[8]{0:T(128)} %bitcast.25), kind=kLoop, calls=%fused_computation.6 | loop fusion | flops 1360 | bytes 996 | tf_op jit(solution)/shard_map/transpose | solution.py:455
  0.9 0.1 copy.9
  1.0 0.1 reshape.30
  1.1 0.4 copy-done
  1.5 0.2 copy.8
  1.7 0.7 broadcast_subtract_fusion
  2.4 0.7 convert_rsqrt_fusion
  3.1 0.1 broadcast_multiply_fusion.fac
  3.1 0.0 copy-start.1
  3.2 1.4 %copy-done.1 = bf16[1,3,8,128,256]{4,3,2,1,0:T(8,128)(2,1)S(1)} copy-done((bf16[1,3,8,128,256]{4,3,2,1,0:T(8,128)(2,1)S(1)}, bf16[1,3,8,128,256]{4,3,2,1,0:T(8,128)(2,1)}, u32[]{:S(2)}) %copy-start.1) | copy-done | bytes 1572888
  4.6 83.1 %levels.1 = f32[8,128]{1,0:T(8,128)S(1)} custom-call(bf16[3,4,64,128]{3,2,1,0:T(8,128)(2,1)S(1)} %bitcast.20, f32[8,128]{1,0:T(8,128)S(1)} %broadcast_multiply_fusion.fac, s32[1,128]{1,0:T(1,128)S(1)} %concatenate.3.ints, bf16[1,3,8,128,256]{4,3,2,1,0:T(8,128)(2,1)S(1)} %copy-done.1), custom_call_target="tpu_custom_call" | custom-call | tf_op jit(solution)/shard_map/levels/pallas_call | solution.py:414
  87.7 0.6 copy.12
  (3 shorter events, 0.1 us)
Async XLA Ops:
  0.0 1.5 %copy-start = (bf16[3,2,128,1024]{3,2,1,0:T(8,128)(2,1)S(1)}, bf16[3,2,128,1024]{3,2,1,0:T(8,128)(2,1)}, u32[]{:S(2)}) copy-start(bf16[3,2,128,1024]{3,2,1,0:T(8,128)(2,1)} %param.6) | copy-start | bytes 4718596
  3.1 1.4 %copy-start.1 = (bf16[1,3,8,128,256]{4,3,2,1,0:T(8,128)(2,1)S(1)}, bf16[1,3,8,128,256]{4,3,2,1,0:T(8,128)(2,1)}, u32[]{:S(2)}) copy-start(bf16[1,3,8,128,256]{4,3,2,1,0:T(8,128)(2,1)} %pool.1) | copy-start | bytes 4718596

commit v4 on v3

v4 whole, which is shorter than its diff:
```python
import jax
import jax.numpy as jnp
from jax import lax
from jax.experimental import pallas as pl
from jax.experimental.pallas import tpu as pltpu
from jax.sharding import PartitionSpec as P

MESH = pl.DeviceIdType.MESH
ANY = pl.BlockSpec(memory_space=pl.ANY)
VMEM = pl.BlockSpec(memory_space=pltpu.VMEM)
BF = jnp.bfloat16
F32 = jnp.float32
WIDE = 144
DEAD = 8 * WIDE


def remote(src, dst, send, recv, d, z, x, c):
    return pltpu.make_async_remote_copy(
        src_ref=src,
        dst_ref=dst,
        send_sem=send,
        recv_sem=recv,
        device_id=(d, z * 4 + x, c),
        device_id_type=MESH,
    )


def arrival(ref, sem):
    return pltpu.make_async_copy(ref, ref, sem)


def turned(rows):
    count = rows.shape[0]
    even = lax.broadcasted_iota(jnp.int32, rows.shape, 0) % 2 == 0
    return jnp.where(even, -pltpu.roll(rows, count - 1, 0), pltpu.roll(rows, 1, 0))


def kernel(
    wsrc, refl, scale, ints, pool, out,
    fac_y, ints_y, wave, field, pool_all, fac_all, ints_all, lists, prod, img, in_x, x_sum, in_yz, done, got,
    l_sem, w_send, w_recv, y_send, y_recv, m_send, m_recv,
    p_send, p_recv, q_send, q_recv, h_send, h_recv, i_send, i_recv, o_send, o_recv, e_sem,
):
    d = lax.axis_index("depth")
    a = lax.axis_index("lat")
    c = lax.axis_index("freq")
    z, x = a // 4, a % 4
    other = 1 - c
    active = z < 6
    side = z // 4
    near = side == c
    source = z // 3
    gives = jnp.logical_and(active, c == source)
    takes = jnp.logical_and(active, c != source)

    def wave_out(i):
        return 3 * c + i // 4, i % 4, side

    def wave_in(i):
        return 4 * c + i // 4, i % 4, source

    def is_me(tz, tx, tc):
        return jnp.logical_and(tz * 4 + tx == a, tc == c)

    def wave_copy(i):
        tz, tx, tc = wave_out(i)
        return remote(
            wsrc.at[i // 4, i % 4], wave.at[a % 16], w_send.at[i], w_recv.at[a % 16], d, tz, tx, tc
        )

    slot = x * 4 + z % 4

    def y_copies(step):
        to = (d + step) % 8
        return (
            remote(fac_y.at[d], fac_y.at[d], y_send.at[0, step], y_recv.at[0, step], to, z, x, c),
            remote(ints_y.at[d], ints_y.at[d], y_send.at[1, step], y_recv.at[1, step], to, z, x, c),
        )

    def list_copies(i):
        tz, tx, tc = wave_out(i)
        return [
            remote(column, whole.at[:, slot], m_send.at[kind, i], m_recv.at[kind, slot], d, tz, tx, tc)
            for kind, column, whole in ((0, fac_y, fac_all), (1, ints_y, ints_all))
        ]

    def ring_copy(way, step, part):
        if way == 0:
            level, to = (d - step + 8) % 8, (d + 1) % 8
        else:
            level, to = (d + step) % 8, (d + 7) % 8
        at = pool_all.at[level, pl.ds(4 * c + 2 * part, 2)]
        i = 2 * step + part
        return remote(at, at, p_send.at[way, i], p_recv.at[way, i], to, z, x, c)

    def share(way, step, part):
        level = (d - 1 - step + 8) % 8 if way == 0 else (d + 1 + step) % 8
        at = pool_all.at[level, pl.ds(4 * c + 2 * part, 2)]
        i = 2 * step + part
        return remote(at, at, q_send.at[way, i], q_recv.at[way, i], d, z, x, other)

    ring = [(way, step, part) for step in range(3) for part in range(2) for way in range(2)]
    ring += [(0, 3, 0), (1, 3, 1)]

    mine = pool.at[0, z % 3]
    here = pltpu.make_async_copy(mine, pool_all.at[d], l_sem.at[0])

    def over(k):
        blocks = pl.ds(4 * other if k == 0 else 4 * c, 4)
        return remote(
            mine.at[blocks], pool_all.at[d, blocks], l_sem.at[3 + k], l_sem.at[5 + k], d, z, x, other
        )

    def came_over(k):
        blocks = pl.ds(4 * c if k == 0 else 4 * other, 4)
        return arrival(pool_all.at[d, blocks], l_sem.at[5 + k])

    def edges(way, parity):
        own, theirs = ((64, 1088), (1024, 0))[way]
        return remote(
            field.at[parity, pl.ds(own, 64)], field.at[parity, pl.ds(theirs, 64)],
            h_send.at[parity, way], h_recv.at[parity, way], d, z, x, other,
        )

    barrier = pltpu.get_barrier_semaphore()

    def greet(d, z, x, c):
        pl.semaphore_signal(barrier, inc=1, device_id=(d, z * 4 + x, c), device_id_type=MESH)

    greet(d, z, x, other)
    for i in range(1, 8):
        greet((d + i) % 8, z, x, c)
    for i in range(1, 4):
        greet(d, z, (x + i) % 4, c)

    @pl.loop(0, 12)
    def _(i):
        @pl.when(jnp.logical_not(is_me(*wave_out(i))))
        def _():
            greet(d, *wave_out(i))

    @pl.when(active)
    def _():
        @pl.loop(0, 16)
        def _(i):
            @pl.when(jnp.logical_not(is_me(*wave_in(i))))
            def _():
                greet(d, *wave_in(i))

    loops = jnp.logical_and(gives, near).astype(jnp.int32)
    fac_y[d] = (1.0 - refl[...]) * scale[...]
    ints_y[d] = ints[...]

    @pl.when(gives)
    def _():
        here.start()

    pl.semaphore_wait(barrier, 11 + 12 - loops + jnp.where(active, 16 - loops, 0))

    @pl.when(gives)
    def _():
        over(0).start()
        over(1).start()

    for step in range(1, 8):
        for copy in y_copies(step):
            copy.start()

    @pl.when(gives)
    def _():
        here.wait()

    @pl.when(takes)
    def _():
        came_over(0).wait()

    @pl.when(active)
    def _():
        for part in range(2):
            ring_copy(0, 0, part).start()
            ring_copy(1, 0, part).start()

    @pl.loop(0, 12)
    def _(i):
        same = is_me(*wave_out(i))

        @pl.when(same)
        def _():
            pltpu.make_async_copy(wsrc.at[i // 4, i % 4], wave.at[a % 16], l_sem.at[1]).start()

        @pl.when(jnp.logical_not(same))
        def _():
            wave_copy(i).start()

    for step in range(1, 8):
        for copy in y_copies(step):
            copy.wait_recv()

    @pl.loop(0, 12)
    def _(i):
        @pl.when(jnp.logical_not(is_me(*wave_out(i))))
        def _():
            for copy in list_copies(i):
                copy.start()

    @pl.when(jnp.logical_and(gives, near))
    def _():
        fac_all[:, slot] = fac_y[...]
        ints_all[:, slot] = ints_y[...]

    def ring_steps(these):
        for way, step, part in these:
            ring_copy(way, step, part).wait_recv()
            if (way, step + 1, part) in ring:
                ring_copy(way, step + 1, part).start()
            share(way, step, part).start()

    @pl.when(active)
    def _():
        ring_steps(ring[:4])

        @pl.loop(0, 16)
        def _(i):
            same = is_me(*wave_in(i))

            @pl.when(same)
            def _():
                arrival(wave.at[i], l_sem.at[1]).wait()

            @pl.when(jnp.logical_not(same))
            def _():
                arrival(wave.at[i], w_recv.at[i]).wait()

            at = pl.ds(pl.multiple_of(64 + 64 * i, 64), 64)
            rows = wave[i]
            field[0, at, :128] = rows
            field[0, at, 128:] = turned(rows.astype(F32)).astype(BF)

        edges(0, 0).start()
        edges(1, 0).start()
        prod[pl.ds(8 * DEAD, 8), :] = jnp.zeros((8, 128), F32)
        ring_steps(ring[4:8])

        @pl.loop(0, 16)
        def _(i):
            @pl.when(jnp.logical_not(is_me(*wave_in(i))))
            def _():
                at = (i % 4) * 4 + i // 4
                arrival(fac_all.at[:, at], m_recv.at[0, at]).wait()
                arrival(ints_all.at[:, at], m_recv.at[1, at]).wait()

        to_scalars = pltpu.make_async_copy(ints_all, lists, l_sem.at[2])
        to_scalars.start()
        ring_steps(ring[8:])
        to_scalars.wait()

        @pl.when(takes)
        def _():
            came_over(1).wait()

        for copy in ring:
            share(*copy).wait_recv()

        batches = ((0, 4), (4, 3), (7, 1))

        def image_copy(batch, step):
            first, count = batches[batch]
            to = (x + step) % 4
            return remote(
                img.at[pl.ds(first, count), pl.ds(4 * to, 4)], in_x.at[step, pl.ds(first, count)],
                i_send.at[batch, step], i_recv.at[batch, step], d, z, to, c,
            )

        def owner_copy(level, k):
            return remote(
                x_sum.at[level, k], in_yz.at[d, z], o_send.at[level, k], o_recv.at[d],
                level, 4 * c + k, x, c,
            )

        def is_owner(level, k):
            return jnp.logical_and(level == d, 4 * c + k == z)

        def send_images(batch):
            for step in range(1, 4):
                image_copy(batch, step).start()

        def hand_in(batch):
            for step in range(1, 4):
                image_copy(batch, step).wait_recv()

            @pl.loop(batches[batch][0], sum(batches[batch]))
            def _(level):
                x_sum[level] = (img[level, pl.ds(4 * x, 4)] + in_x[1, level]) + (
                    in_x[2, level] + in_x[3, level]
                )
                for k in range(4):
                    @pl.when(is_owner(level, k))
                    def _():
                        in_yz[d, z] = x_sum[level, k]

                    @pl.when(jnp.logical_not(is_owner(level, k)))
                    def _():
                        owner_copy(level, k).start()

        def group(level, now, g):
            later = 1 - now
            for m in range(16):
                new = []
                for r in (2 * m, 2 * m + 1):
                    block = 4 * g + r // 8
                    at = (block % 4) * 4 + block // 4
                    parts = []
                    for k in range(10):
                        parts.append(prod[pl.ds(lists[level, at, 0, k * 8 + r % 8], 8), :])
                    while len(parts) > 1:
                        parts = [sum(parts[i + 1 : i + 2], parts[i]) for i in range(0, len(parts), 2)]
                    row = parts[0] * fac_all[level, at, r % 8 : r % 8 + 1, :]
                    img[level, at, r % 8 : r % 8 + 1, :] = jnp.sum(row * row, axis=0, keepdims=True)
                    new.append(row)
                pair = jnp.concatenate(new, 0)
                at = pl.ds(pl.multiple_of(64 + 256 * g + 16 * m, 16), 16)
                field[later, at, :128] = pair.astype(BF)
                field[later, at, 128:] = turned(pair).astype(BF)

        @pl.loop(0, 8)
        def _(level):
            now = level % 2
            for way in range(2):
                edges(way, now).wait()
            for p in range(4):
                b0, b1 = pool_all[level, 2 * p], pool_all[level, 2 * p + 1]
                weights = jnp.concatenate(
                    [
                        jnp.concatenate([b0[:, :128], b1[:, :128]], 1),
                        jnp.concatenate([b0[:, 128:], b1[:, 128:]], 1),
                    ],
                    0,
                )
                product = jnp.dot(field[now], weights, preferred_element_type=F32)
                for k in range(2):
                    rows = pl.ds((2 * p + k) * 8 * WIDE, 8 * WIDE)
                    prod[rows, :] = product[:, 128 * k : 128 * k + 128]

            @pl.loop(0, 2)
            def _(i):
                group(level, now, 3 * i)

            @pl.when(level < 7)
            def _():
                for way in range(2):
                    edges(way, 1 - now).start()

            @pl.loop(1, 3)
            def _(g):
                group(level, now, g)

            for batch in range(2):
                @pl.when(level == sum(batches[batch]) - 1)
                def _():
                    send_images(batch)

            @pl.when(level == 5)
            def _():
                hand_in(0)

        send_images(2)
        hand_in(1)
        hand_in(2)

        for batch in range(3):
            for step in range(1, 4):
                image_copy(batch, step).wait_send()

        @pl.loop(0, 8)
        def _(level):
            for k in range(4):
                @pl.when(jnp.logical_not(is_owner(level, k)))
                def _():
                    owner_copy(level, k).wait_send()

    echo = remote(done, got, e_sem.at[0], e_sem.at[1], d, z, x, other)

    @pl.when(near)
    def _():
        total = jnp.zeros((8, 128), F32)
        for fd in range(8):
            @pl.when(jnp.logical_and(active, d == fd))
            def _():
                arrival(in_yz.at[fd, pl.ds(0, 5)], o_recv.at[fd]).wait()

            @pl.when(jnp.logical_not(jnp.logical_and(active, d == fd)))
            def _():
                arrival(in_yz.at[fd, pl.ds(0, 6)], o_recv.at[fd]).wait()

        for fd in range(8):
            for fz in range(6):
                total = total + in_yz[fd, fz]
        done[...] = total / 768.0
        echo.start()
        out[...] = done[...]
        echo.wait_send()

    @pl.when(jnp.logical_not(near))
    def _():
        echo.wait_recv()
        out[...] = got[...]

    for step in range(1, 8):
        for copy in y_copies(step):
            copy.wait_send()

    @pl.loop(0, 12)
    def _(i):
        @pl.when(jnp.logical_not(is_me(*wave_out(i))))
        def _():
            wave_copy(i).wait_send()
            for copy in list_copies(i):
                copy.wait_send()

    @pl.when(gives)
    def _():
        over(0).wait_send()
        over(1).wait_send()

    @pl.when(active)
    def _():
        for copy in ring:
            ring_copy(*copy).wait_send()
            share(*copy).wait_send()


def run(wsrc, refl, scale, ints, pool):
    dma = pltpu.SemaphoreType.DMA
    vmem = pltpu.VMEM
    return pl.pallas_call(
        kernel,
        out_shape=jax.ShapeDtypeStruct((8, 128), F32),
        in_specs=[VMEM, VMEM, VMEM, VMEM, ANY],
        out_specs=VMEM,
        scratch_shapes=[
            vmem((8, 8, 128), F32),
            vmem((8, 1, 128), jnp.int32),
            vmem((16, 64, 128), BF),
            vmem((2, 8 * WIDE, 256), BF),
            vmem((8, 8, 128, 256), BF),
            vmem((8, 16, 8, 128), F32),
            vmem((8, 16, 1, 128), jnp.int32),
            pltpu.SMEM((8, 16, 1, 128), jnp.int32),
            vmem((8 * DEAD + 8, 128), F32),
            vmem((8, 16, 8, 128), F32),
            vmem((4, 8, 4, 8, 128), F32),
            vmem((8, 4, 8, 128), F32),
            vmem((8, 8, 8, 128), F32),
            vmem((8, 128), F32),
            vmem((8, 128), F32),
            dma((7,)), dma((12,)), dma((16,)), dma((2, 8)), dma((2, 8)), dma((2, 12)), dma((2, 16)),
            dma((2, 8)), dma((2, 8)), dma((2, 8)), dma((2, 8)),
            dma((2, 2)), dma((2, 2)), dma((3, 4)), dma((3, 4)), dma((8, 4)), dma((8,)), dma((2,)),
        ],
        compiler_params=pltpu.CompilerParams(
            has_side_effects=True, collective_id=1, vmem_limit_bytes=60 * 2**20
        ),
        name="levels",
    )(wsrc, refl, scale, ints, pool)


def per_device(surface, refl, pool, tile_ids, block_ids, counts):
    d = lax.axis_index("depth")
    first = 128 * (lax.axis_index("lat") // 16)
    own = lax.dynamic_slice_in_dim(surface, d * 16, 16, 2)
    own = own.reshape(3, 2, 4, 4, 8, 128)
    wsrc = jnp.transpose(own, (0, 2, 4, 3, 1, 5)).reshape(3, 4, 64, 128)
    scale = jnp.broadcast_to((1.0 / jnp.sqrt(counts[0].astype(F32)))[:, None], (8, 128))
    live = jnp.arange(10)[None, :] < counts[0][:, None]
    slots = 8 * jnp.where(live, block_ids[0] * WIDE + (tile_ids[0] - first + 8) % 256, DEAD)
    ints = jnp.concatenate([slots.T.reshape(1, 80), jnp.zeros((1, 48), jnp.int32)], 1)
    return run(wsrc, refl.reshape(8, 128), scale, ints.astype(jnp.int32), pool).reshape(1, 1024)


def solution(mesh):
    placed = (
        P("freq", None, None, "lat"),
        P("depth", "lat"),
        P("depth", "freq", None, None, None),
        P("depth", "lat", None),
        P("depth", "lat", None),
        P("depth", "lat"),
    )
    return jax.shard_map(
        per_device, mesh=mesh, in_specs=placed, out_specs=P("depth", "lat"), check_vma=False
    )
```

time: 88.5 us -> 82.2 us (0.929)
  Pallas kernels: 83.1 us -> 76.9 us
    pallas_call x1, Pallas kernels: 83.1 us -> 76.9 us  [run(): pl.pallas_call(kernel, out_shape=jax.ShapeDtypeStruct((8, 128), F32), in_...]
    unnamed x6 -> x4, local copies, waits for them, and re-layouts: 2.42 us -> 1.3 us
where the time goes in v4:
time: 82.2 us; the launch traced here: 82 us
  Pallas kernels  76.9 us (94%)
  local copies, waits for them, and re-layouts  3.55 us (4%)
  other arithmetic  1.55 us (2%)
    pallas_call x1, Pallas kernels, run(): pl.pallas_call(kernel, out_shape=jax.ShapeDtypeStruct((8, 128), F32), in_...  76.9 us

profile of v4, /device:TPU:57, one launch (start us, length us, event | category | flops | bytes accessed | tf_op | source)
XLA Modules:
  0.0 82.0 jit_solution(15642315927025039191)
XLA Ops:
  0.0 0.0 copy-start
  0.0 0.9 %fusion.4 = s32[10,8]{0,1:T(8,128)S(1)} fusion(s32[1,8,10]{2,1,0:T(8,128)} %param.10, s32[1,8,10]{2,1,0:T(8,128)} %param.9, s32[]{:T(128)S(6)} %mul.22, s32[8]{0:T(128)} %bitcast.25), kind=kLoop, calls=%fused_computation.7 | loop fusion | flops 1440 | bytes 996 | tf_op jit(solution)/shard_map/transpose | solution.py:476
  0.9 0.1 copy.9
  1.0 0.1 reshape.31
  1.1 0.5 concatenate.3.ints
  1.6 0.0 copy-done
  1.6 0.9 %copy.8 = bf16[3,4,8,4,2,128]{5,4,3,2,1,0:T(2,128)(2,1)} copy(bf16[3,4,8,4,2,128]{5,2,3,1,4,0:T(8,128)(2,1)S(1)} %bitcast.21) | data formatting | bytes 393216 | tf_op jit(solution)/shard_map/transpose | solution.py:472
  2.5 0.7 convert_rsqrt_fusion
  3.2 0.7 broadcast_in_dim.5.scale
  3.9 76.9 %levels.1 = f32[8,128]{1,0:T(8,128)} custom-call(bf16[3,4,64,128]{3,2,1,0:T(8,128)(2,1)} %bitcast.22, f32[8,128]{1,0:T(8,128)} %bitcast.24, f32[8,128]{1,0:T(8,128)} %broadcast_in_dim.5.scale, s32[1,128]{1,0:T(1,128)} %concatenate.3.ints, bf16[1,3,8,128,256]{4,3,2,1,0:T(8,128)(2,1)} %pool.1), custom_call_target="tpu_custom_call" | custom-call | tf_op jit(solution)/shard_map/levels/pallas_call | solution.py:435
  80.7 1.3 %copy.12 = f32[1,1024]{1,0:T(1,128)} copy(f32[1,1024]{1,0:T(1,128)} %bitcast.23) | data formatting | bytes 8192
  (2 shorter events, 0.0 us)
Async XLA Ops:
  0.0 1.6 %copy-start = (bf16[3,2,128,1024]{3,2,1,0:T(8,128)(2,1)S(1)}, bf16[3,2,128,1024]{3,2,1,0:T(8,128)(2,1)}, u32[]{:S(2)}) copy-start(bf16[3,2,128,1024]{3,2,1,0:T(8,128)(2,1)} %param.6) | copy-start | bytes 4718596

commit v5 on v4

--- a/solution.py
+++ b/solution.py
@@ -36,10 +36,10 @@
 
 
 def kernel(
-    wsrc, refl, scale, ints, pool, out,
-    fac_y, ints_y, wave, field, pool_all, fac_all, ints_all, lists, prod, img, in_x, x_sum, in_yz, done, got,
+    wsrc, refl, tiles, blocks, counts, pool, out,
+    draft, fac_y, ints_y, wave, field, pool_all, fac_all, ints_all, lists, prod, img, in_x, x_sum, in_yz,
     l_sem, w_send, w_recv, y_send, y_recv, m_send, m_recv,
-    p_send, p_recv, q_send, q_recv, h_send, h_recv, i_send, i_recv, o_send, o_recv, e_sem,
+    f_send, p_send, p_recv, q_send, q_recv, h_send, h_recv, i_send, i_recv, o_send, o_recv,
 ):
     d = lax.axis_index("depth")
     a = lax.axis_index("lat")
@@ -84,6 +84,8 @@
             for kind, column, whole in ((0, fac_y, fac_all), (1, ints_y, ints_all))
         ]
 
+    mine = pool.at[0, z % 3]
+
     def ring_copy(way, step, part):
         if way == 0:
             level, to = (d - step + 8) % 8, (d + 1) % 8
@@ -99,21 +101,20 @@
         i = 2 * step + part
         return remote(at, at, q_send.at[way, i], q_recv.at[way, i], d, z, x, other)
 
+    def first_copy(way, part, tc):
+        blocks_here = pl.ds(4 * tc + 2 * part, 2)
+        to = (d + 1) % 8 if way == 0 else (d + 7) % 8
+        return remote(
+            mine.at[blocks_here], pool_all.at[d, blocks_here],
+            f_send.at[way, 2 * part + (tc == c).astype(jnp.int32)], p_recv.at[way, part], to, z, x, tc,
+        )
+
     ring = [(way, step, part) for step in range(3) for part in range(2) for way in range(2)]
     ring += [(0, 3, 0), (1, 3, 1)]
 
-    mine = pool.at[0, z % 3]
     here = pltpu.make_async_copy(mine, pool_all.at[d], l_sem.at[0])
 
-    def over(k):
-        blocks = pl.ds(4 * other if k == 0 else 4 * c, 4)
-        return remote(
-            mine.at[blocks], pool_all.at[d, blocks], l_sem.at[3 + k], l_sem.at[5 + k], d, z, x, other
-        )
-
-    def came_over(k):
-        blocks = pl.ds(4 * c if k == 0 else 4 * other, 4)
-        return arrival(pool_all.at[d, blocks], l_sem.at[5 + k])
+    over = remote(mine, pool_all.at[d], l_sem.at[3], l_sem.at[4], d, z, x, other)
 
     def edges(way, parity):
         own, theirs = ((64, 1088), (1024, 0))[way]
@@ -128,6 +129,8 @@
         pl.semaphore_signal(barrier, inc=1, device_id=(d, z * 4 + x, c), device_id_type=MESH)
 
     greet(d, z, x, other)
+    greet((d + 1) % 8, z, x, other)
+    greet((d + 7) % 8, z, x, other)
     for i in range(1, 8):
         greet((d + i) % 8, z, x, c)
     for i in range(1, 4):
@@ -148,37 +151,37 @@
                 greet(d, *wave_in(i))
 
     loops = jnp.logical_and(gives, near).astype(jnp.int32)
-    fac_y[d] = (1.0 - refl[...]) * scale[...]
-    ints_y[d] = ints[...]
+    lane = lax.broadcasted_iota(jnp.int32, (1, 128), 1)
+    draft[...] = jnp.zeros((8, 128), jnp.int32)
+    draft[:, :10] = 8 * (blocks[...] * WIDE + (tiles[...] - 128 * side + 8) % 256)
+    line = jnp.zeros((1, 128), jnp.int32)
+    for r in range(8):
+        live = counts[0, r]
+        fac_y[d, r : r + 1, :] = (1.0 - refl[r : r + 1, :]) * (
+            1.0 / jnp.sqrt(jnp.full((1, 128), live, jnp.int32).astype(F32))
+        )
+        slots = jnp.where(lane < live, draft[r : r + 1, :], 8 * DEAD)
+        slots = jnp.where(lane < 10, slots, 0)
+        line = line + (slots if r == 0 else pltpu.roll(slots, 10 * r, 1))
+    ints_y[d] = line
 
     @pl.when(gives)
     def _():
         here.start()
 
-    pl.semaphore_wait(barrier, 11 + 12 - loops + jnp.where(active, 16 - loops, 0))
+    pl.semaphore_wait(barrier, 13 + 12 - loops + jnp.where(active, 16 - loops, 0))
 
     @pl.when(gives)
     def _():
-        over(0).start()
-        over(1).start()
+        for part in range(2):
+            for tc in (c, other):
+                for way in range(2):
+                    first_copy(way, part, tc).start()
+        over.start()
 
     for step in range(1, 8):
         for copy in y_copies(step):
             copy.start()
-
-    @pl.when(gives)
-    def _():
-        here.wait()
-
-    @pl.when(takes)
-    def _():
-        came_over(0).wait()
-
-    @pl.when(active)
-    def _():
-        for part in range(2):
-            ring_copy(0, 0, part).start()
-            ring_copy(1, 0, part).start()
 
     @pl.loop(0, 12)
     def _(i):
@@ -254,9 +257,13 @@
         ring_steps(ring[8:])
         to_scalars.wait()
 
+        @pl.when(gives)
+        def _():
+            here.wait()
+
         @pl.when(takes)
         def _():
-            came_over(1).wait()
+            over.wait_recv()
 
         for copy in ring:
             share(*copy).wait_recv()
@@ -271,10 +278,10 @@
                 i_send.at[batch, step], i_recv.at[batch, step], d, z, to, c,
             )
 
-        def owner_copy(level, k):
+        def owner_copy(level, k, tc):
             return remote(
-                x_sum.at[level, k], in_yz.at[d, z], o_send.at[level, k], o_recv.at[d],
-                level, 4 * c + k, x, c,
+                x_sum.at[level, k], in_yz.at[d, z], o_send.at[level, 2 * k + (tc == c).astype(jnp.int32)],
+                o_recv.at[d], level, 4 * c + k, x, tc,
             )
 
         def is_owner(level, k):
@@ -300,7 +307,9 @@
 
                     @pl.when(jnp.logical_not(is_owner(level, k)))
                     def _():
-                        owner_copy(level, k).start()
+                        owner_copy(level, k, c).start()
+
+                    owner_copy(level, k, other).start()
 
         def group(level, now, g):
             later = 1 - now
@@ -311,7 +320,7 @@
                     at = (block % 4) * 4 + block // 4
                     parts = []
                     for k in range(10):
-                        parts.append(prod[pl.ds(lists[level, at, 0, k * 8 + r % 8], 8), :])
+                        parts.append(prod[pl.ds(lists[level, at, 0, r % 8 * 10 + k], 8), :])
                     while len(parts) > 1:
                         parts = [sum(parts[i + 1 : i + 2], parts[i]) for i in range(0, len(parts), 2)]
                     row = parts[0] * fac_all[level, at, r % 8 : r % 8 + 1, :]
@@ -376,34 +385,29 @@
             for k in range(4):
                 @pl.when(jnp.logical_not(is_owner(level, k)))
                 def _():
-                    owner_copy(level, k).wait_send()
-
-    echo = remote(done, got, e_sem.at[0], e_sem.at[1], d, z, x, other)
-
-    @pl.when(near)
-    def _():
-        total = jnp.zeros((8, 128), F32)
-        for fd in range(8):
-            @pl.when(jnp.logical_and(active, d == fd))
-            def _():
-                arrival(in_yz.at[fd, pl.ds(0, 5)], o_recv.at[fd]).wait()
-
-            @pl.when(jnp.logical_not(jnp.logical_and(active, d == fd)))
-            def _():
-                arrival(in_yz.at[fd, pl.ds(0, 6)], o_recv.at[fd]).wait()
-
-        for fd in range(8):
-            for fz in range(6):
-                total = total + in_yz[fd, fz]
-        done[...] = total / 768.0
-        echo.start()
-        out[...] = done[...]
-        echo.wait_send()
-
-    @pl.when(jnp.logical_not(near))
-    def _():
-        echo.wait_recv()
-        out[...] = got[...]
+                    owner_copy(level, k, c).wait_send()
+
+                owner_copy(level, k, other).wait_send()
+
+    own = jnp.logical_and(active, near)
+    total = jnp.zeros((8, 128), F32)
+    for fd in range(8):
+        local = jnp.logical_and(own, d == fd)
+
+        @pl.when(local)
+        def _():
+            arrival(in_yz.at[fd, pl.ds(0, 5)], o_recv.at[fd]).wait()
+
+        @pl.when(jnp.logical_not(local))
+        def _():
+            arrival(in_yz.at[fd, pl.ds(0, 6)], o_recv.at[fd]).wait()
+
+    for fd in range(8):
+        for fz in range(6):
+            total = total + in_yz[fd, fz]
+    total = total / 768.0
+    for r in range(8):
+        out[:, 128 * r : 128 * r + 128] = total[r : r + 1, :]
 
     for step in range(1, 8):
         for copy in y_copies(step):
@@ -419,25 +423,30 @@
 
     @pl.when(gives)
     def _():
-        over(0).wait_send()
-        over(1).wait_send()
+        over.wait_send()
+        for part in range(2):
+            for tc in (c, other):
+                for way in range(2):
+                    first_copy(way, part, tc).wait_send()
 
     @pl.when(active)
     def _():
-        for copy in ring:
-            ring_copy(*copy).wait_send()
-            share(*copy).wait_send()
-
-
-def run(wsrc, refl, scale, ints, pool):
+        for way, step, part in ring:
+            if step:
+                ring_copy(way, step, part).wait_send()
+            share(way, step, part).wait_send()
+
+
+def run(wsrc, refl, tiles, blocks, counts, pool):
     dma = pltpu.SemaphoreType.DMA
     vmem = pltpu.VMEM
     return pl.pallas_call(
         kernel,
-        out_shape=jax.ShapeDtypeStruct((8, 128), F32),
-        in_specs=[VMEM, VMEM, VMEM, VMEM, ANY],
+        out_shape=jax.ShapeDtypeStruct((1, 1024), F32),
+        in_specs=[VMEM, VMEM, VMEM, VMEM, pl.BlockSpec(memory_space=pltpu.SMEM), ANY],
         out_specs=VMEM,
         scratch_shapes=[
+            vmem((8, 128), jnp.int32),
             vmem((8, 8, 128), F32),
             vmem((8, 1, 128), jnp.int32),
             vmem((16, 64, 128), BF),
@@ -451,30 +460,23 @@
             vmem((4, 8, 4, 8, 128), F32),
             vmem((8, 4, 8, 128), F32),
             vmem((8, 8, 8, 128), F32),
-            vmem((8, 128), F32),
-            vmem((8, 128), F32),
-            dma((7,)), dma((12,)), dma((16,)), dma((2, 8)), dma((2, 8)), dma((2, 12)), dma((2, 16)),
-            dma((2, 8)), dma((2, 8)), dma((2, 8)), dma((2, 8)),
-            dma((2, 2)), dma((2, 2)), dma((3, 4)), dma((3, 4)), dma((8, 4)), dma((8,)), dma((2,)),
+            dma((5,)), dma((12,)), dma((16,)), dma((2, 8)), dma((2, 8)), dma((2, 12)), dma((2, 16)),
+            dma((2, 4)), dma((2, 8)), dma((2, 8)), dma((2, 8)), dma((2, 8)),
+            dma((2, 2)), dma((2, 2)), dma((3, 4)), dma((3, 4)), dma((8, 8)), dma((8,)),
         ],
         compiler_params=pltpu.CompilerParams(
             has_side_effects=True, collective_id=1, vmem_limit_bytes=60 * 2**20
         ),
         name="levels",
-    )(wsrc, refl, scale, ints, pool)
+    )(wsrc, refl, tiles, blocks, counts, pool)
 
 
 def per_device(surface, refl, pool, tile_ids, block_ids, counts):
     d = lax.axis_index("depth")
-    first = 128 * (lax.axis_index("lat") // 16)
     own = lax.dynamic_slice_in_dim(surface, d * 16, 16, 2)
     own = own.reshape(3, 2, 4, 4, 8, 128)
     wsrc = jnp.transpose(own, (0, 2, 4, 3, 1, 5)).reshape(3, 4, 64, 128)
-    scale = jnp.broadcast_to((1.0 / jnp.sqrt(counts[0].astype(F32)))[:, None], (8, 128))
-    live = jnp.arange(10)[None, :] < counts[0][:, None]
-    slots = 8 * jnp.where(live, block_ids[0] * WIDE + (tile_ids[0] - first + 8) % 256, DEAD)
-    ints = jnp.concatenate([slots.T.reshape(1, 80), jnp.zeros((1, 48), jnp.int32)], 1)
-    return run(wsrc, refl.reshape(8, 128), scale, ints.astype(jnp.int32), pool).reshape(1, 1024)
+    return run(wsrc, refl.reshape(8, 128), tile_ids[0], block_ids[0], counts, pool)
 
 
 def solution(mesh):

time: 82.2 us -> 82.9 us (level)
  Pallas kernels: 76.9 us -> 78.7 us
  other arithmetic: 1.55 us -> 0 us
    pallas_call x1, Pallas kernels: 76.9 us -> 78.7 us  [run(): pl.pallas_call(kernel, out_shape=jax.ShapeDtypeStruct((1, 1024), F32), in...]
    unnamed x4, local copies, waits for them, and re-layouts: 1.3 us -> 2.7 us
    transpose x1 -> x0, other arithmetic: 0.89 us -> none  [per_device(): slots.T.reshape(1, 80)]
where the time goes in v5:
time: 82.9 us; the launch traced here: 82.3 us
  Pallas kernels  78.7 us (95%)
  local copies, waits for them, and re-layouts  3.59 us (4%)
    pallas_call x1, Pallas kernels, run(): pl.pallas_call(kernel, out_shape=jax.ShapeDtypeStruct((1, 1024), F32), in...  78.7 us
    unnamed x4, local copies, waits for them, and re-layouts  2.7 us

profile of v5, /device:TPU:57, one launch (start us, length us, event | category | flops | bytes accessed | tf_op | source)
XLA Modules:
  0.0 82.3 jit_solution(9523369174532699390)
XLA Ops:
  0.0 0.0 copy-start
  0.0 1.4 %copy-done = bf16[3,2,128,1024]{3,2,1,0:T(8,128)(2,1)S(1)} copy-done((bf16[3,2,128,1024]{3,2,1,0:T(8,128)(2,1)S(1)}, bf16[3,2,128,1024]{3,2,1,0:T(8,128)(2,1)}, u32[]{:S(2)}) %copy-start) | copy-done | bytes 1572888
  1.5 0.9 %copy.7 = bf16[3,4,8,4,2,128]{5,4,3,2,1,0:T(2,128)(2,1)} copy(bf16[3,4,8,4,2,128]{5,2,3,1,4,0:T(8,128)(2,1)S(1)} %bitcast.12) | data formatting | bytes 393216 | tf_op jit(solution)/shard_map/transpose | solution.py:478
  2.3 78.7 %levels.1 = f32[1,1024]{1,0:T(1,128)} custom-call(bf16[3,4,64,128]{3,2,1,0:T(8,128)(2,1)} %bitcast.13, f32[8,128]{1,0:T(8,128)} %bitcast.14, s32[8,10]{1,0:T(8,128)} %bitcast.15, s32[8,10]{1,0:T(8,128)} %bitcast.16, s32[1,8]{1,0:T(1,128)} %counts.1, bf16[1,3,8,128,256]{4,3,2,1,0:T(8,128)(2,1)} %pool.1), custom_call_target="tpu_custom_call" | custom-call | tf_op jit(solution)/shard_map/levels/pallas_call | solution.py:443
  81.1 1.3 %copy.10 = f32[1,1024]{1,0:T(1,128)} copy(f32[1,1024]{1,0:T(1,128)} %levels.1) | data formatting | bytes 8192
  (2 shorter events, 0.0 us)
Async XLA Ops:
  0.0 1.4 %copy-start = (bf16[3,2,128,1024]{3,2,1,0:T(8,128)(2,1)S(1)}, bf16[3,2,128,1024]{3,2,1,0:T(8,128)(2,1)}, u32[]{:S(2)}) copy-start(bf16[3,2,128,1024]{3,2,1,0:T(8,128)(2,1)} %param.6) | copy-start | bytes 4718596

commit v6 on v5

--- a/solution.py
+++ b/solution.py
@@ -36,8 +36,8 @@
 
 
 def kernel(
-    wsrc, refl, tiles, blocks, counts, pool, out,
-    draft, fac_y, ints_y, wave, field, pool_all, fac_all, ints_all, lists, prod, img, in_x, x_sum, in_yz,
+    surface, refl, tiles, blocks, counts, pool, out,
+    raw, mixed, wsrc, draft, fac_y, ints_y, wave, field, pool_all, fac_all, ints_all, lists, prod, img, in_x, x_sum, in_yz,
     l_sem, w_send, w_recv, y_send, y_recv, m_send, m_recv,
     f_send, p_send, p_recv, q_send, q_recv, h_send, h_recv, i_send, i_recv, o_send, o_recv,
 ):
@@ -151,6 +151,13 @@
                 greet(d, *wave_in(i))
 
     loops = jnp.logical_and(gives, near).astype(jnp.int32)
+    fetch = pltpu.make_async_copy(surface.at[:, :, pl.ds(16 * d, 16), :], raw, l_sem.at[5])
+    fetch.start()
+
+    @pl.when(gives)
+    def _():
+        here.start()
+
     lane = lax.broadcasted_iota(jnp.int32, (1, 128), 1)
     draft[...] = jnp.zeros((8, 128), jnp.int32)
     draft[:, :10] = 8 * (blocks[...] * WIDE + (tiles[...] - 128 * side + 8) % 256)
@@ -165,9 +172,19 @@
         line = line + (slots if r == 0 else pltpu.roll(slots, 10 * r, 1))
     ints_y[d] = line
 
-    @pl.when(gives)
-    def _():
-        here.start()
+    fetch.wait()
+
+    @pl.loop(0, 3)
+    def _(f):
+        for part in range(2):
+            rows = raw[f, part].astype(F32)
+            for tx in range(4):
+                for t in range(8):
+                    at = pl.ds(256 * f + 64 * tx + 8 * t + part, 4, stride=2)
+                    mixed[at, :] = rows[4 * tx : 4 * tx + 4, 128 * t : 128 * t + 128]
+        for tx in range(4):
+            at = pl.ds(pl.multiple_of(256 * f + 64 * tx, 64), 64)
+            wsrc[f, tx] = mixed[at, :].astype(BF)
 
     pl.semaphore_wait(barrier, 13 + 12 - loops + jnp.where(active, 16 - loops, 0))
 
@@ -242,7 +259,7 @@
         edges(0, 0).start()
         edges(1, 0).start()
         prod[pl.ds(8 * DEAD, 8), :] = jnp.zeros((8, 128), F32)
-        ring_steps(ring[4:8])
+        ring_steps(ring[4:12])
 
         @pl.loop(0, 16)
         def _(i):
@@ -254,7 +271,7 @@
 
         to_scalars = pltpu.make_async_copy(ints_all, lists, l_sem.at[2])
         to_scalars.start()
-        ring_steps(ring[8:])
+        ring_steps(ring[12:])
         to_scalars.wait()
 
         @pl.when(gives)
@@ -268,7 +285,7 @@
         for copy in ring:
             share(*copy).wait_recv()
 
-        batches = ((0, 4), (4, 3), (7, 1))
+        batches = ((0, 3), (3, 3), (6, 1), (7, 1))
 
         def image_copy(batch, step):
             first, count = batches[batch]
@@ -363,20 +380,20 @@
             def _(g):
                 group(level, now, g)
 
-            for batch in range(2):
+            for batch in range(4):
                 @pl.when(level == sum(batches[batch]) - 1)
                 def _():
                     send_images(batch)
 
-            @pl.when(level == 5)
-            def _():
-                hand_in(0)
-
-        send_images(2)
-        hand_in(1)
+            for batch in range(2):
+                @pl.when(level == 4 + 2 * batch)
+                def _():
+                    hand_in(batch)
+
         hand_in(2)
-
-        for batch in range(3):
+        hand_in(3)
+
+        for batch in range(4):
             for step in range(1, 4):
                 image_copy(batch, step).wait_send()
 
@@ -405,9 +422,7 @@
     for fd in range(8):
         for fz in range(6):
             total = total + in_yz[fd, fz]
-    total = total / 768.0
-    for r in range(8):
-        out[:, 128 * r : 128 * r + 128] = total[r : r + 1, :]
+    out[...] = total
 
     for step in range(1, 8):
         for copy in y_copies(step):
@@ -437,15 +452,18 @@
             share(way, step, part).wait_send()
 
 
-def run(wsrc, refl, tiles, blocks, counts, pool):
+def run(surface, refl, tiles, blocks, counts, pool):
     dma = pltpu.SemaphoreType.DMA
     vmem = pltpu.VMEM
     return pl.pallas_call(
         kernel,
-        out_shape=jax.ShapeDtypeStruct((1, 1024), F32),
-        in_specs=[VMEM, VMEM, VMEM, VMEM, pl.BlockSpec(memory_space=pltpu.SMEM), ANY],
+        out_shape=jax.ShapeDtypeStruct((8, 128), F32),
+        in_specs=[ANY, VMEM, VMEM, VMEM, pl.BlockSpec(memory_space=pltpu.SMEM), ANY],
         out_specs=VMEM,
         scratch_shapes=[
+            vmem((3, 2, 16, 1024), BF),
+            vmem((768, 128), F32),
+            vmem((3, 4, 64, 128), BF),
             vmem((8, 128), jnp.int32),
             vmem((8, 8, 128), F32),
             vmem((8, 1, 128), jnp.int32),
@@ -460,23 +478,20 @@
             vmem((4, 8, 4, 8, 128), F32),
             vmem((8, 4, 8, 128), F32),
             vmem((8, 8, 8, 128), F32),
-            dma((5,)), dma((12,)), dma((16,)), dma((2, 8)), dma((2, 8)), dma((2, 12)), dma((2, 16)),
+            dma((6,)), dma((12,)), dma((16,)), dma((2, 8)), dma((2, 8)), dma((2, 12)), dma((2, 16)),
             dma((2, 4)), dma((2, 8)), dma((2, 8)), dma((2, 8)), dma((2, 8)),
-            dma((2, 2)), dma((2, 2)), dma((3, 4)), dma((3, 4)), dma((8, 8)), dma((8,)),
+            dma((2, 2)), dma((2, 2)), dma((4, 4)), dma((4, 4)), dma((8, 8)), dma((8,)),
         ],
         compiler_params=pltpu.CompilerParams(
             has_side_effects=True, collective_id=1, vmem_limit_bytes=60 * 2**20
         ),
         name="levels",
-    )(wsrc, refl, tiles, blocks, counts, pool)
+    )(surface, refl, tiles, blocks, counts, pool)
 
 
 def per_device(surface, refl, pool, tile_ids, block_ids, counts):
-    d = lax.axis_index("depth")
-    own = lax.dynamic_slice_in_dim(surface, d * 16, 16, 2)
-    own = own.reshape(3, 2, 4, 4, 8, 128)
-    wsrc = jnp.transpose(own, (0, 2, 4, 3, 1, 5)).reshape(3, 4, 64, 128)
-    return run(wsrc, refl.reshape(8, 128), tile_ids[0], block_ids[0], counts, pool)
+    image = run(surface, refl.reshape(8, 128), tile_ids[0], block_ids[0], counts, pool)
+    return (image / 768.0).reshape(1, 1024)
 
 
 def solution(mesh):

time: 82.9 us -> 81.3 us (0.981)
  local copies, waits for them, and re-layouts: 3.59 us -> 0 us
  other arithmetic: 0 us -> 1.28 us
  Pallas kernels: 78.7 us -> 79.8 us
    unnamed x4 -> x0, local copies, waits for them, and re-layouts: 2.7 us -> none
    div x0 -> x1, other arithmetic: none -> 1.28 us  [per_device(): return (image / 768.0).reshape(1, 1024)]
    pallas_call x1, Pallas kernels: 78.7 us -> 79.8 us  [run(): pl.pallas_call(kernel, out_shape=jax.ShapeDtypeStruct((8, 128), F32), in_...]
    transpose x1 -> x0, local copies, waits for them, and re-layouts: 0.88 us -> none  [per_device(): wsrc = jnp.transpose(own, (0, 2, 4, 3, 1, 5)).reshape(3, 4, 64, 128)]
where the time goes in v6:
time: 81.3 us; the launch traced here: 81.1 us
  Pallas kernels  79.8 us (98%)
  other arithmetic  1.28 us (2%)
    pallas_call x1, Pallas kernels, run(): pl.pallas_call(kernel, out_shape=jax.ShapeDtypeStruct((8, 128), F32), in_...  79.8 us

profile of v6, /device:TPU:57, one launch (start us, length us, event | category | flops | bytes accessed | tf_op | source)
XLA Modules:
  0.0 81.1 jit_solution(1892430699463346709)
XLA Ops:
  0.0 79.8 %levels.1 = f32[8,128]{1,0:T(8,128)} custom-call(bf16[3,2,128,1024]{3,2,1,0:T(8,128)(2,1)} %surface.1, f32[8,128]{1,0:T(8,128)} %bitcast.4, s32[8,10]{1,0:T(8,128)} %bitcast.5, s32[8,10]{1,0:T(8,128)} %bitcast.6, s32[1,8]{1,0:T(1,128)} %counts.1, bf16[1,3,8,128,256]{4,3,2,1,0:T(8,128)(2,1)} %pool.1), custom_call_target="tpu_custom_call" | custom-call | tf_op jit(solution)/shard_map/levels/pallas_call | solution.py:458
  79.8 1.3 %broadcast_multiply_fusion = f32[8,128]{1,0:T(8,128)} fusion(f32[8,128]{1,0:T(8,128)} %levels.1), kind=kLoop, calls=%fused_computation | loop fusion | flops 1024 | bytes 8192 | tf_op jit(solution)/shard_map/div | solution.py:494

commit v7 on v4

--- a/solution.py
+++ b/solution.py
@@ -36,8 +36,8 @@
 
 
 def kernel(
-    wsrc, refl, scale, ints, pool, out,
-    fac_y, ints_y, wave, field, pool_all, fac_all, ints_all, lists, prod, img, in_x, x_sum, in_yz, done, got,
+    surface, refl, tiles, blocks, counts, pool, out,
+    raw, mixed, wsrc, draft, fac_y, ints_y, wave, field, pool_all, fac_all, ints_all, lists, prod, img, in_x, x_sum, in_yz, done, got,
     l_sem, w_send, w_recv, y_send, y_recv, m_send, m_recv,
     p_send, p_recv, q_send, q_recv, h_send, h_recv, i_send, i_recv, o_send, o_recv, e_sem,
 ):
@@ -84,6 +84,8 @@
             for kind, column, whole in ((0, fac_y, fac_all), (1, ints_y, ints_all))
         ]
 
+    mine = pool.at[0, z % 3]
+
     def ring_copy(way, step, part):
         if way == 0:
             level, to = (d - step + 8) % 8, (d + 1) % 8
@@ -102,18 +104,17 @@
     ring = [(way, step, part) for step in range(3) for part in range(2) for way in range(2)]
     ring += [(0, 3, 0), (1, 3, 1)]
 
-    mine = pool.at[0, z % 3]
     here = pltpu.make_async_copy(mine, pool_all.at[d], l_sem.at[0])
 
     def over(k):
-        blocks = pl.ds(4 * other if k == 0 else 4 * c, 4)
+        blocks_here = pl.ds(4 * other if k == 0 else 4 * c, 4)
         return remote(
-            mine.at[blocks], pool_all.at[d, blocks], l_sem.at[3 + k], l_sem.at[5 + k], d, z, x, other
+            mine.at[blocks_here], pool_all.at[d, blocks_here],
+            l_sem.at[3 + k], l_sem.at[6 + k], d, z, x, other,
         )
 
     def came_over(k):
-        blocks = pl.ds(4 * c if k == 0 else 4 * other, 4)
-        return arrival(pool_all.at[d, blocks], l_sem.at[5 + k])
+        return arrival(pool_all.at[d, pl.ds(4 * c if k == 0 else 4 * other, 4)], l_sem.at[6 + k])
 
     def edges(way, parity):
         own, theirs = ((64, 1088), (1024, 0))[way]
@@ -148,12 +149,40 @@
                 greet(d, *wave_in(i))
 
     loops = jnp.logical_and(gives, near).astype(jnp.int32)
-    fac_y[d] = (1.0 - refl[...]) * scale[...]
-    ints_y[d] = ints[...]
+    fetch = pltpu.make_async_copy(surface.at[:, :, pl.ds(16 * d, 16), :], raw, l_sem.at[5])
+    fetch.start()
 
     @pl.when(gives)
     def _():
         here.start()
+
+    lane = lax.broadcasted_iota(jnp.int32, (1, 128), 1)
+    draft[...] = jnp.zeros((8, 128), jnp.int32)
+    draft[:, :10] = 8 * (blocks[...] * WIDE + (tiles[...] - 128 * side + 8) % 256)
+    line = jnp.zeros((1, 128), jnp.int32)
+    for r in range(8):
+        live = counts[0, r]
+        fac_y[d, r : r + 1, :] = (1.0 - refl[r : r + 1, :]) * (
+            1.0 / jnp.sqrt(jnp.full((1, 128), live, jnp.int32).astype(F32))
+        )
+        slots = jnp.where(lane < live, draft[r : r + 1, :], 8 * DEAD)
+        slots = jnp.where(lane < 10, slots, 0)
+        line = line + (slots if r == 0 else pltpu.roll(slots, 10 * r, 1))
+    ints_y[d] = line
+
+    fetch.wait()
+
+    @pl.loop(0, 3)
+    def _(f):
+        for part in range(2):
+            rows = raw[f, part].astype(F32)
+            for tx in range(4):
+                for t in range(8):
+                    at = pl.ds(256 * f + 64 * tx + 8 * t + part, 4, stride=2)
+                    mixed[at, :] = rows[4 * tx : 4 * tx + 4, 128 * t : 128 * t + 128]
+        for tx in range(4):
+            at = pl.ds(pl.multiple_of(256 * f + 64 * tx, 64), 64)
+            wsrc[f, tx] = mixed[at, :].astype(BF)
 
     pl.semaphore_wait(barrier, 11 + 12 - loops + jnp.where(active, 16 - loops, 0))
 
@@ -161,24 +190,21 @@
     def _():
         over(0).start()
         over(1).start()
+        here.wait()
+
+    @pl.when(takes)
+    def _():
+        came_over(0).wait()
+
+    @pl.when(active)
+    def _():
+        for part in range(2):
+            for way in range(2):
+                ring_copy(way, 0, part).start()
 
     for step in range(1, 8):
         for copy in y_copies(step):
             copy.start()
-
-    @pl.when(gives)
-    def _():
-        here.wait()
-
-    @pl.when(takes)
-    def _():
-        came_over(0).wait()
-
-    @pl.when(active)
-    def _():
-        for part in range(2):
-            ring_copy(0, 0, part).start()
-            ring_copy(1, 0, part).start()
 
     @pl.loop(0, 12)
     def _(i):
@@ -239,7 +265,7 @@
         edges(0, 0).start()
         edges(1, 0).start()
         prod[pl.ds(8 * DEAD, 8), :] = jnp.zeros((8, 128), F32)
-        ring_steps(ring[4:8])
+        ring_steps(ring[4:12])
 
         @pl.loop(0, 16)
         def _(i):
@@ -251,7 +277,7 @@
 
         to_scalars = pltpu.make_async_copy(ints_all, lists, l_sem.at[2])
         to_scalars.start()
-        ring_steps(ring[8:])
+        ring_steps(ring[12:])
         to_scalars.wait()
 
         @pl.when(takes)
@@ -261,7 +287,7 @@
         for copy in ring:
             share(*copy).wait_recv()
 
-        batches = ((0, 4), (4, 3), (7, 1))
+        batches = ((0, 5), (5, 2), (7, 1))
 
         def image_copy(batch, step):
             first, count = batches[batch]
@@ -311,7 +337,7 @@
                     at = (block % 4) * 4 + block // 4
                     parts = []
                     for k in range(10):
-                        parts.append(prod[pl.ds(lists[level, at, 0, k * 8 + r % 8], 8), :])
+                        parts.append(prod[pl.ds(lists[level, at, 0, r % 8 * 10 + k], 8), :])
                     while len(parts) > 1:
                         parts = [sum(parts[i + 1 : i + 2], parts[i]) for i in range(0, len(parts), 2)]
                     row = parts[0] * fac_all[level, at, r % 8 : r % 8 + 1, :]
@@ -354,18 +380,13 @@
             def _(g):
                 group(level, now, g)
 
-            for batch in range(2):
+            for batch in range(3):
                 @pl.when(level == sum(batches[batch]) - 1)
                 def _():
                     send_images(batch)
 
-            @pl.when(level == 5)
-            def _():
-                hand_in(0)
-
-        send_images(2)
-        hand_in(1)
-        hand_in(2)
+        for batch in range(3):
+            hand_in(batch)
 
         for batch in range(3):
             for step in range(1, 4):
@@ -384,20 +405,22 @@
     def _():
         total = jnp.zeros((8, 128), F32)
         for fd in range(8):
-            @pl.when(jnp.logical_and(active, d == fd))
+            local = jnp.logical_and(active, d == fd)
+
+            @pl.when(local)
             def _():
                 arrival(in_yz.at[fd, pl.ds(0, 5)], o_recv.at[fd]).wait()
 
-            @pl.when(jnp.logical_not(jnp.logical_and(active, d == fd)))
+            @pl.when(jnp.logical_not(local))
             def _():
                 arrival(in_yz.at[fd, pl.ds(0, 6)], o_recv.at[fd]).wait()
 
         for fd in range(8):
             for fz in range(6):
                 total = total + in_yz[fd, fz]
-        done[...] = total / 768.0
+        done[...] = total
         echo.start()
-        out[...] = done[...]
+        out[...] = total
         echo.wait_send()
 
     @pl.when(jnp.logical_not(near))
@@ -424,20 +447,24 @@
 
     @pl.when(active)
     def _():
-        for copy in ring:
-            ring_copy(*copy).wait_send()
-            share(*copy).wait_send()
-
-
-def run(wsrc, refl, scale, ints, pool):
+        for way, step, part in ring:
+            ring_copy(way, step, part).wait_send()
+            share(way, step, part).wait_send()
+
+
+def run(surface, refl, tiles, blocks, counts, pool):
     dma = pltpu.SemaphoreType.DMA
     vmem = pltpu.VMEM
     return pl.pallas_call(
         kernel,
         out_shape=jax.ShapeDtypeStruct((8, 128), F32),
-        in_specs=[VMEM, VMEM, VMEM, VMEM, ANY],
+        in_specs=[ANY, VMEM, VMEM, VMEM, pl.BlockSpec(memory_space=pltpu.SMEM), ANY],
         out_specs=VMEM,
         scratch_shapes=[
+            vmem((3, 2, 16, 1024), BF),
+            vmem((768, 128), F32),
+            vmem((3, 4, 64, 128), BF),
+            vmem((8, 128), jnp.int32),
             vmem((8, 8, 128), F32),
             vmem((8, 1, 128), jnp.int32),
             vmem((16, 64, 128), BF),
@@ -453,7 +480,7 @@
             vmem((8, 8, 8, 128), F32),
             vmem((8, 128), F32),
             vmem((8, 128), F32),
-            dma((7,)), dma((12,)), dma((16,)), dma((2, 8)), dma((2, 8)), dma((2, 12)), dma((2, 16)),
+            dma((8,)), dma((12,)), dma((16,)), dma((2, 8)), dma((2, 8)), dma((2, 12)), dma((2, 16)),
             dma((2, 8)), dma((2, 8)), dma((2, 8)), dma((2, 8)),
             dma((2, 2)), dma((2, 2)), dma((3, 4)), dma((3, 4)), dma((8, 4)), dma((8,)), dma((2,)),
         ],
@@ -461,20 +488,12 @@
             has_side_effects=True, collective_id=1, vmem_limit_bytes=60 * 2**20
         ),
         name="levels",
-    )(wsrc, refl, scale, ints, pool)
+    )(surface, refl, tiles, blocks, counts, pool)
 
 
 def per_device(surface, refl, pool, tile_ids, block_ids, counts):
-    d = lax.axis_index("depth")
-    first = 128 * (lax.axis_index("lat") // 16)
-    own = lax.dynamic_slice_in_dim(surface, d * 16, 16, 2)
-    own = own.reshape(3, 2, 4, 4, 8, 128)
-    wsrc = jnp.transpose(own, (0, 2, 4, 3, 1, 5)).reshape(3, 4, 64, 128)
-    scale = jnp.broadcast_to((1.0 / jnp.sqrt(counts[0].astype(F32)))[:, None], (8, 128))
-    live = jnp.arange(10)[None, :] < counts[0][:, None]
-    slots = 8 * jnp.where(live, block_ids[0] * WIDE + (tile_ids[0] - first + 8) % 256, DEAD)
-    ints = jnp.concatenate([slots.T.reshape(1, 80), jnp.zeros((1, 48), jnp.int32)], 1)
-    return run(wsrc, refl.reshape(8, 128), scale, ints.astype(jnp.int32), pool).reshape(1, 1024)
+    image = run(surface, refl.reshape(8, 128), tile_ids[0], block_ids[0], counts, pool)
+    return (image / 768.0).reshape(1, 1024)
 
 
 def solution(mesh):

time: 82.2 us -> 78.7 us (0.957)
  local copies, waits for them, and re-layouts: 3.55 us -> 0 us
    unnamed x4 -> x0, local copies, waits for them, and re-layouts: 1.3 us -> none
    div x0 -> x1, other arithmetic: none -> 1.28 us  [per_device(): return (image / 768.0).reshape(1, 1024)]
    transpose x2 -> x0, local copies, waits for them, and re-layouts: 0.96 us -> none  [the longest x1 0.88 us: per_device(): wsrc = jnp.transpose(own, (0, 2, 4, 3, 1, 5)).reshape(3, 4, 64, 128)]
    transpose x1 -> x0, other arithmetic: 0.89 us -> none  [per_device(): slots.T.reshape(1, 80)]
where the time goes in v7:
time: 78.7 us; the launch traced here: 78.1 us
  Pallas kernels  76.9 us (98%)
  other arithmetic  1.28 us (2%)
    pallas_call x1, Pallas kernels, run(): pl.pallas_call(kernel, out_shape=jax.ShapeDtypeStruct((8, 128), F32), in_...  76.9 us

profile of v7, /device:TPU:57, one launch (start us, length us, event | category | flops | bytes accessed | tf_op | source)
XLA Modules:
  0.0 78.1 jit_solution(805408325329202497)
XLA Ops:
  0.0 76.9 %levels.1 = f32[8,128]{1,0:T(8,128)} custom-call(bf16[3,2,128,1024]{3,2,1,0:T(8,128)(2,1)} %surface.1, f32[8,128]{1,0:T(8,128)} %bitcast.4, s32[8,10]{1,0:T(8,128)} %bitcast.5, s32[8,10]{1,0:T(8,128)} %bitcast.6, s32[1,8]{1,0:T(1,128)} %counts.1, bf16[1,3,8,128,256]{4,3,2,1,0:T(8,128)(2,1)} %pool.1), custom_call_target="tpu_custom_call" | custom-call | tf_op jit(solution)/shard_map/levels/pallas_call | solution.py:458
  76.9 1.3 %broadcast_multiply_fusion = f32[8,128]{1,0:T(8,128)} fusion(f32[8,128]{1,0:T(8,128)} %levels.1), kind=kLoop, calls=%fused_computation | loop fusion | flops 1024 | bytes 8192 | tf_op jit(solution)/shard_map/div | solution.py:496

commit v8 on v7

--- a/solution.py
+++ b/solution.py
@@ -39,7 +39,7 @@
     surface, refl, tiles, blocks, counts, pool, out,
     raw, mixed, wsrc, draft, fac_y, ints_y, wave, field, pool_all, fac_all, ints_all, lists, prod, img, in_x, x_sum, in_yz, done, got,
     l_sem, w_send, w_recv, y_send, y_recv, m_send, m_recv,
-    p_send, p_recv, q_send, q_recv, h_send, h_recv, i_send, i_recv, o_send, o_recv, e_sem,
+    p_send, p_recv, q_send, q_recv, g_send, g_recv, t_send, t_recv, h_send, h_recv, i_send, i_recv, o_send, o_recv, e_sem,
 ):
     d = lax.axis_index("depth")
     a = lax.axis_index("lat")
@@ -79,42 +79,65 @@
 
     def list_copies(i):
         tz, tx, tc = wave_out(i)
+        soon, late = pl.ds(0, 2), pl.ds(2, 6)
         return [
-            remote(column, whole.at[:, slot], m_send.at[kind, i], m_recv.at[kind, slot], d, tz, tx, tc)
-            for kind, column, whole in ((0, fac_y, fac_all), (1, ints_y, ints_all))
+            remote(column, target, m_send.at[kind, i], m_recv.at[kind, slot], d, tz, tx, tc)
+            for kind, (column, target) in enumerate(
+                (
+                    (fac_y.at[soon], fac_all.at[soon, slot]),
+                    (ints_y, ints_all.at[:, slot]),
+                    (fac_y.at[late], fac_all.at[late, slot]),
+                )
+            )
         ]
 
     mine = pool.at[0, z % 3]
+    unit = x % 2 * 2 + c
+    across = (x + 1) % 2 * 2 + c
 
     def ring_copy(way, step, part):
         if way == 0:
             level, to = (d - step + 8) % 8, (d + 1) % 8
         else:
             level, to = (d + step) % 8, (d + 7) % 8
-        at = pool_all.at[level, pl.ds(4 * c + 2 * part, 2)]
+        at = pool_all.at[level, pl.ds(2 * unit + part, 1)]
         i = 2 * step + part
         return remote(at, at, p_send.at[way, i], p_recv.at[way, i], to, z, x, c)
 
+    def came(way, step):
+        return (d - 1 - step + 8) % 8 if way == 0 else (d + 1 + step) % 8
+
     def share(way, step, part):
-        level = (d - 1 - step + 8) % 8 if way == 0 else (d + 1 + step) % 8
-        at = pool_all.at[level, pl.ds(4 * c + 2 * part, 2)]
+        at = pool_all.at[came(way, step), pl.ds(2 * unit + part, 1)]
         i = 2 * step + part
         return remote(at, at, q_send.at[way, i], q_recv.at[way, i], d, z, x, other)
 
+    def cross(way, step, part):
+        at = pool_all.at[came(way, step), pl.ds(2 * unit + part, 1)]
+        i, to = 2 * step + part, (x + 1 + 2 * part) % 4
+        return remote(at, at, g_send.at[way, i], g_recv.at[way, i], d, z, to, c)
+
+    def pass_on(way, step, part):
+        at = pool_all.at[came(way, step), pl.ds(2 * across + part, 1)]
+        i = 2 * step + part
+        return arrival(at, g_recv.at[way, i]), remote(
+            at, at, t_send.at[way, i], t_recv.at[way, i], d, z, x, other
+        )
+
     ring = [(way, step, part) for step in range(3) for part in range(2) for way in range(2)]
     ring += [(0, 3, 0), (1, 3, 1)]
 
     here = pltpu.make_async_copy(mine, pool_all.at[d], l_sem.at[0])
 
     def over(k):
-        blocks_here = pl.ds(4 * other if k == 0 else 4 * c, 4)
+        blocks_here = pl.ds(4 * ((x + k) % 2), 4)
         return remote(
             mine.at[blocks_here], pool_all.at[d, blocks_here],
             l_sem.at[3 + k], l_sem.at[6 + k], d, z, x, other,
         )
 
     def came_over(k):
-        return arrival(pool_all.at[d, pl.ds(4 * c if k == 0 else 4 * other, 4)], l_sem.at[6 + k])
+        return arrival(pool_all.at[d, pl.ds(4 * ((x + k) % 2), 4)], l_sem.at[6 + k])
 
     def edges(way, parity):
         own, theirs = ((64, 1088), (1024, 0))[way]
@@ -226,8 +249,14 @@
     def _(i):
         @pl.when(jnp.logical_not(is_me(*wave_out(i))))
         def _():
-            for copy in list_copies(i):
+            for copy in list_copies(i)[:2]:
                 copy.start()
+
+    @pl.loop(0, 12)
+    def _(i):
+        @pl.when(jnp.logical_not(is_me(*wave_out(i))))
+        def _():
+            list_copies(i)[2].start()
 
     @pl.when(jnp.logical_and(gives, near))
     def _():
@@ -239,7 +268,14 @@
             ring_copy(way, step, part).wait_recv()
             if (way, step + 1, part) in ring:
                 ring_copy(way, step + 1, part).start()
+            cross(way, step, part).start()
             share(way, step, part).start()
+
+    def cross_steps(these):
+        for copy in these:
+            came_across, onward = pass_on(*copy)
+            came_across.wait()
+            onward.start()
 
     @pl.when(active)
     def _():
@@ -265,19 +301,23 @@
         edges(0, 0).start()
         edges(1, 0).start()
         prod[pl.ds(8 * DEAD, 8), :] = jnp.zeros((8, 128), F32)
-        ring_steps(ring[4:12])
+        ring_steps(ring[4:8])
+        cross_steps(ring[:4])
+        ring_steps(ring[8:12])
+        cross_steps(ring[4:8])
 
         @pl.loop(0, 16)
         def _(i):
             @pl.when(jnp.logical_not(is_me(*wave_in(i))))
             def _():
                 at = (i % 4) * 4 + i // 4
-                arrival(fac_all.at[:, at], m_recv.at[0, at]).wait()
+                arrival(fac_all.at[pl.ds(0, 2), at], m_recv.at[0, at]).wait()
                 arrival(ints_all.at[:, at], m_recv.at[1, at]).wait()
 
         to_scalars = pltpu.make_async_copy(ints_all, lists, l_sem.at[2])
         to_scalars.start()
         ring_steps(ring[12:])
+        cross_steps(ring[8:])
         to_scalars.wait()
 
         @pl.when(takes)
@@ -286,6 +326,7 @@
 
         for copy in ring:
             share(*copy).wait_recv()
+            pass_on(*copy)[1].wait_recv()
 
         batches = ((0, 5), (5, 2), (7, 1))
 
@@ -351,6 +392,16 @@
         @pl.loop(0, 8)
         def _(level):
             now = level % 2
+
+            @pl.when(level == 2)
+            def _():
+                @pl.loop(0, 16)
+                def _(i):
+                    @pl.when(jnp.logical_not(is_me(*wave_in(i))))
+                    def _():
+                        at = (i % 4) * 4 + i // 4
+                        arrival(fac_all.at[pl.ds(2, 6), at], m_recv.at[2, at]).wait()
+
             for way in range(2):
                 edges(way, now).wait()
             for p in range(4):
@@ -450,6 +501,8 @@
         for way, step, part in ring:
             ring_copy(way, step, part).wait_send()
             share(way, step, part).wait_send()
+            cross(way, step, part).wait_send()
+            pass_on(way, step, part)[1].wait_send()
 
 
 def run(surface, refl, tiles, blocks, counts, pool):
@@ -480,7 +533,8 @@
             vmem((8, 8, 8, 128), F32),
             vmem((8, 128), F32),
             vmem((8, 128), F32),
-            dma((8,)), dma((12,)), dma((16,)), dma((2, 8)), dma((2, 8)), dma((2, 12)), dma((2, 16)),
+            dma((8,)), dma((12,)), dma((16,)), dma((2, 8)), dma((2, 8)), dma((3, 12)), dma((3, 16)),
+            dma((2, 8)), dma((2, 8)), dma((2, 8)), dma((2, 8)),
             dma((2, 8)), dma((2, 8)), dma((2, 8)), dma((2, 8)),
             dma((2, 2)), dma((2, 2)), dma((3, 4)), dma((3, 4)), dma((8, 4)), dma((8,)), dma((2,)),
         ],

time: 78.7 us -> 77.8 us (0.989)
  no operation moved by 1% of the time
where the time goes in v8:
time: 77.8 us; the launch traced here: 77.6 us
  Pallas kernels  76.3 us (98%)
  other arithmetic  1.28 us (2%)
    pallas_call x1, Pallas kernels, run(): pl.pallas_call(kernel, out_shape=jax.ShapeDtypeStruct((8, 128), F32), in_...  76.3 us

profile of v8, /device:TPU:57, one launch (start us, length us, event | category | flops | bytes accessed | tf_op | source)
XLA Modules:
  0.0 77.6 jit_solution(4092679340880292845)
XLA Ops:
  0.0 76.3 %levels.1 = f32[8,128]{1,0:T(8,128)} custom-call(bf16[3,2,128,1024]{3,2,1,0:T(8,128)(2,1)} %surface.1, f32[8,128]{1,0:T(8,128)} %bitcast.4, s32[8,10]{1,0:T(8,128)} %bitcast.5, s32[8,10]{1,0:T(8,128)} %bitcast.6, s32[1,8]{1,0:T(1,128)} %counts.1, bf16[1,3,8,128,256]{4,3,2,1,0:T(8,128)(2,1)} %pool.1), custom_call_target="tpu_custom_call" | custom-call | tf_op jit(solution)/shard_map/levels/pallas_call | solution.py:511
  76.3 1.3 %broadcast_multiply_fusion = f32[8,128]{1,0:T(8,128)} fusion(f32[8,128]{1,0:T(8,128)} %levels.1), kind=kLoop, calls=%fused_computation | loop fusion | flops 1024 | bytes 8192 | tf_op jit(solution)/shard_map/div | solution.py:550

commit v9 on v8

--- a/solution.py
+++ b/solution.py
@@ -107,8 +107,11 @@
     def came(way, step):
         return (d - 1 - step + 8) % 8 if way == 0 else (d + 1 + step) % 8
 
+    def both(first, step, part):
+        return pl.ds(2 * first, 2) if step < 3 else pl.ds(2 * first + part, 1)
+
     def share(way, step, part):
-        at = pool_all.at[came(way, step), pl.ds(2 * unit + part, 1)]
+        at = pool_all.at[came(way, step), both(unit, step, part)]
         i = 2 * step + part
         return remote(at, at, q_send.at[way, i], q_recv.at[way, i], d, z, x, other)
 
@@ -119,13 +122,15 @@
 
     def pass_on(way, step, part):
         at = pool_all.at[came(way, step), pl.ds(2 * across + part, 1)]
+        pair = pool_all.at[came(way, step), both(across, step, part)]
         i = 2 * step + part
         return arrival(at, g_recv.at[way, i]), remote(
-            at, at, t_send.at[way, i], t_recv.at[way, i], d, z, x, other
+            pair, pair, t_send.at[way, i], t_recv.at[way, i], d, z, x, other
         )
 
     ring = [(way, step, part) for step in range(3) for part in range(2) for way in range(2)]
     ring += [(0, 3, 0), (1, 3, 1)]
+    whole = [copy for copy in ring if copy[1] == 3 or copy[2] == 1]
 
     here = pltpu.make_async_copy(mine, pool_all.at[d], l_sem.at[0])
 
@@ -157,7 +162,7 @@
     for i in range(1, 4):
         greet(d, z, (x + i) % 4, c)
 
-    @pl.loop(0, 12)
+    @pl.loop(0, 12, unroll=True)
     def _(i):
         @pl.when(jnp.logical_not(is_me(*wave_out(i))))
         def _():
@@ -165,7 +170,7 @@
 
     @pl.when(active)
     def _():
-        @pl.loop(0, 16)
+        @pl.loop(0, 16, unroll=True)
         def _(i):
             @pl.when(jnp.logical_not(is_me(*wave_in(i))))
             def _():
@@ -269,13 +274,15 @@
             if (way, step + 1, part) in ring:
                 ring_copy(way, step + 1, part).start()
             cross(way, step, part).start()
-            share(way, step, part).start()
+            if (way, step, part) in whole:
+                share(way, step, part).start()
 
     def cross_steps(these):
         for copy in these:
             came_across, onward = pass_on(*copy)
             came_across.wait()
-            onward.start()
+            if copy in whole:
+                onward.start()
 
     @pl.when(active)
     def _():
@@ -324,7 +331,7 @@
         def _():
             came_over(1).wait()
 
-        for copy in ring:
+        for copy in whole:
             share(*copy).wait_recv()
             pass_on(*copy)[1].wait_recv()
 
@@ -427,7 +434,7 @@
                 for way in range(2):
                     edges(way, 1 - now).start()
 
-            @pl.loop(1, 3)
+            @pl.loop(1, 3, unroll=True)
             def _(g):
                 group(level, now, g)
 
@@ -500,9 +507,10 @@
     def _():
         for way, step, part in ring:
             ring_copy(way, step, part).wait_send()
-            share(way, step, part).wait_send()
             cross(way, step, part).wait_send()
-            pass_on(way, step, part)[1].wait_send()
+        for copy in whole:
+            share(*copy).wait_send()
+            pass_on(*copy)[1].wait_send()
 
 
 def run(surface, refl, tiles, blocks, counts, pool):

time: 77.8 us -> 77.4 us (level)
  no operation moved by 1% of the time
where the time goes in v9:
time: 77.4 us; the launch traced here: 77.2 us
  Pallas kernels  75.9 us (98%)
  other arithmetic  1.28 us (2%)
    pallas_call x1, Pallas kernels, run(): pl.pallas_call(kernel, out_shape=jax.ShapeDtypeStruct((8, 128), F32), in_...  75.9 us

profile of v9, /device:TPU:57, one launch (start us, length us, event | category | flops | bytes accessed | tf_op | source)
XLA Modules:
  0.0 77.2 jit_solution(11426273119910381295)
XLA Ops:
  0.0 75.9 %levels.1 = f32[8,128]{1,0:T(8,128)} custom-call(bf16[3,2,128,1024]{3,2,1,0:T(8,128)(2,1)} %surface.1, f32[8,128]{1,0:T(8,128)} %bitcast.4, s32[8,10]{1,0:T(8,128)} %bitcast.5, s32[8,10]{1,0:T(8,128)} %bitcast.6, s32[1,8]{1,0:T(1,128)} %counts.1, bf16[1,3,8,128,256]{4,3,2,1,0:T(8,128)(2,1)} %pool.1), custom_call_target="tpu_custom_call" | custom-call | tf_op jit(solution)/shard_map/levels/pallas_call | solution.py:519
  75.9 1.3 %broadcast_multiply_fusion = f32[8,128]{1,0:T(8,128)} fusion(f32[8,128]{1,0:T(8,128)} %levels.1), kind=kLoop, calls=%fused_computation | loop fusion | flops 1024 | bytes 8192 | tf_op jit(solution)/shard_map/div | solution.py:558
